TPU v7x, 32 devices: a whole 2x2x4 slice. The times are simulated.
32 devices in a mesh: chan: 8 (over z, y), tm: 4 (over x, core).
Axes of the slice: x: 2, y: 2, z: 4, core: 2. Of those that a mesh axis runs over, the one named last changes fastest.
Arguments:
- recording: bfloat16 [4096, 8192], P('chan', 'tm'), may hold values from -6 to 6
- band_taps: bfloat16 [3, 255], replicated, may hold values from -0.375 to 0.375
- channel_gain: float32 [4096], P('chan'), may hold values from 0.25 to 2
- range_test: bfloat16 [8192, 64], P('tm'), may hold values from -0.0625 to 0.0625
- corange_test: bfloat16 [64, 4096], P(None, 'chan'), may hold values from -0.09375 to 0.09375
- core_left: bfloat16 [128, 4096], P(None, 'chan'), may hold values from -0.09375 to 0.09375
- core_right: bfloat16 [8192, 128], P('tm'), may hold values from -0.0625 to 0.0625
Outputs:
- strain_rate: bfloat16 [3, 4096, 8192], P(None, 'chan', 'tm')
- range_sketch: float32 [3, 4096, 64], P(None, 'chan')
- corange_sketch: float32 [3, 64, 8192], P(None, None, 'tm')
- core_sketch: float32 [3, 128, 128], replicated
All inputs are finite; a program needn't handle non-finite values.
Results may differ from a plain program's by a relative error of at most 0.0052.
Values may be sent and summed in bfloat16 or wider, within the bound.
A program may use at most 64 MiB of HBM per device.

v0:
```python
import jax
import jax.numpy as jnp
from jax import lax
from jax.sharding import PartitionSpec as P


def padded_2(block, sides, width):
    for axis, dim in sides:
        count = lax.axis_size(axis)
        forward = [(i, i + 1) for i in range(count - 1)]
        backward = [(target, source) for source, target in forward]
        low = lax.ppermute(
            lax.slice_in_dim(block, block.shape[dim] - width, None, axis=dim), axis, forward
        )
        high = lax.ppermute(lax.slice_in_dim(block, 0, width, axis=dim), axis, backward)
        block = jnp.concatenate([low, block, high], axis=dim)
    return block


def on_device(recording, band_taps, channel_gain, range_test, corange_test, core_left, core_right):
    tap_count = band_taps.shape[1]
    half_width = tap_count // 2
    channels, samples = recording.shape
    padded = padded_2(recording, (("tm", 1),), half_width)
    padded = jnp.pad(padded, ((0, 0), (0, 256 - 2 * half_width)))
    blocks = samples // 128
    lead_block = padded[:, :samples].reshape(channels, blocks, 128)
    mid_block = padded[:, 128 : samples + 128].reshape(channels, blocks, 128)
    tail_block = padded[:, 256 : samples + 256].reshape(channels, blocks, 128)
    windows = jnp.concatenate([lead_block, mid_block, tail_block], axis=2)
    window_pos = lax.broadcasted_iota(jnp.int32, (384, 128), 0)
    output_pos = lax.broadcasted_iota(jnp.int32, (384, 128), 1)
    offset = window_pos - output_pos
    inside = (offset >= 0) & (offset < tap_count)
    picked = jnp.take(band_taps, jnp.clip(offset, 0, tap_count - 1), axis=1)
    toeplitz = jnp.where(inside[None], picked, jnp.zeros_like(picked))
    band_count = band_taps.shape[0]
    filtered = jnp.einsum("cnw,bwo->bcno", windows, toeplitz, preferred_element_type=jnp.float32)
    filtered = filtered.reshape(band_count, channels, samples).astype(jnp.bfloat16)
    rimmed = padded_2(filtered, (("chan", 1),), 1)
    difference = rimmed[:, 2:].astype(jnp.float32) - rimmed[:, :-2].astype(jnp.float32)
    strain_rate = (channel_gain[None, :, None] * difference).astype(jnp.bfloat16)
    range_part = jnp.einsum(
        "bct,tk->bck", strain_rate, range_test, preferred_element_type=jnp.float32
    )
    corange_part = jnp.einsum(
        "lc,bct->blt", corange_test, strain_rate, preferred_element_type=jnp.float32
    )
    high = lax.Precision.HIGHEST
    projected = jnp.einsum(
        "bct,ts->bcs", strain_rate, core_right, preferred_element_type=jnp.float32
    )
    range_sketch, projected_sum = lax.psum((range_part, projected), "tm")
    corange_sketch = lax.psum(corange_part, "chan")
    core_term = jnp.einsum(
        "rc,bcs->brs", core_left.astype(jnp.float32), projected_sum, precision=high
    )
    core_sketch = lax.psum(core_term, "chan")
    return (strain_rate, range_sketch, corange_sketch, core_sketch)


def solution(mesh):
    in_specs = (
        P("chan", "tm"),
        P(),
        P("chan"),
        P("tm", None),
        P(None, "chan"),
        P(None, "chan"),
        P("tm", None),
    )
    out_specs = (P(None, "chan", "tm"), P(None, "chan", None), P(None, None, "tm"), P())
    return jax.shard_map(
        on_device, mesh=mesh, in_specs=in_specs, out_specs=out_specs, check_vma=False
    )
```

profile of v0, /device:TPU:0, one launch (start us, length us, event | category | flops | bytes accessed | tf_op | source)
XLA Modules:
  0.0 424.9 jit_solution(13206108507670665187)
XLA Ops:
  7.2 2.9 copy.20
  10.9 2.4 collective-permute-start
  15.4 170.7 %gather_fusion = bf16[49152,3]{1,0:T(8,128)(2,1)} fusion(bf16[3,255]{0,1:T(8,128)(2,1)S(1)} %copy.18, s32[49152]{0:T(1024)S(1)} %fusion.16), kind=kCustom, calls=%fused_computation | custom fusion | bytes 786432 | tf_op jit(solution)/shard_map/jit(_take)/gather | solution.py:35
  186.2 16.1 %copy.19 = bf16[384,128,3]{0,1,2:T(8,128)(2,1)S(1)} copy(bf16[384,128,3]{2,1,0:T(8,128)(2,1)} %bitcast.43) | data formatting | bytes 589824 | tf_op jit(solution)/shard_map/jit(_take)/gather | solution.py:35
  202.4 11.3 %concatenate.21 = bf16[512,2302]{0,1:T(8,128)(2,1)} concatenate(bf16[512,127]{0,1:T(8,128)(2,1)S(1)} %collective-permute-done, bf16[512,2048]{0,1:T(8,128)(2,1)S(1)} %copy.20, bf16[512,127]{0,1:T(8,128)(2,1)S(1)} %collective-permute-done.1), dimensions={1} | concatenate | bytes 4714496 | tf_op jit(solution)/shard_map/concatenate | solution.py:16
  213.7 3.1 pad_slice_fusion
  216.8 3.9 copy.27
  220.7 2.5 pad_maximum_fusion.3
  223.2 4.1 copy.26
  227.3 3.9 copy.25
  231.2 6.9 %fusion.5 = bf16[3,128,512,16]{2,1,3,0:T(8,128)(2,1)} fusion(bf16[512,16,128]{2,0,1:T(8,128)(2,1)S(1)} %copy-done.2, bf16[512,16,128]{2,0,1:T(8,128)(2,1)} %copy.26, bf16[512,16,128]{2,0,1:T(8,128)(2,1)} %copy.25, bf16[384,128,3]{0,1,2:T(8,128)(2,1)S(1)} %copy.19, pred[384,128]{0,1:T(8,128)(4,1)S(1)} %get-tuple-element.23, ...), kind=kOutput, calls=%fused_computation.10 | convolution fusion | flops 2438234112 | bytes 12976128 | tf_op jit(solution)/shard_map/cnw,bwo->bcno/dot_general | solution.py:38
  238.1 8.9 %copy.29 = bf16[3,512,2048]{2,1,0:T(8,128)(2,1)} copy(bf16[3,512,2048]{1,2,0:T(8,128)(2,1)} %bitcast.47) | data formatting | bytes 12582912 | tf_op jit(solution)/shard_map/convert_element_type | solution.py:39
  248.0 4.3 %collective-permute-start.3 = (bf16[3,1,2048]{2,1,0:T(2,128)(2,1)S(1)}, bf16[3,1,2048]{2,1,0:T(2,128)(2,1)S(1)}, u32[]{:S(2)}, u32[]{:S(2)}) collective-permute-start(bf16[3,1,2048]{2,1,0:T(2,128)(2,1)S(1)} %get-tuple-element.17), channel_id=1, source_target_pairs={{0,4},{4,8},{8,12},{12,16},{16,20},{20,24},{24,28},{1,5},{5,9},{9,... | collective-permute-start | bytes 36872 | tf_op jit(solution)/shard_map/ppermute | solution.py:12
  253.8 4.4 %collective-permute-done.2 = bf16[3,1,2048]{2,1,0:T(2,128)(2,1)S(1)} collective-permute-done((bf16[3,1,2048]{2,1,0:T(2,128)(2,1)S(1)}, bf16[3,1,2048]{2,1,0:T(2,128)(2,1)S(1)}, u32[]{:S(2)}, u32[]{:S(2)}) %collective-permute-start.2) | collective-permute-done | bytes 12320 | tf_op jit(solution)/shard_map/ppermute | solution.py:15
  258.2 8.3 %multiply_convert_fusion = bf16[3,512,2048]{2,1,0:T(8,128)(2,1)S(1)} fusion(bf16[3,512,2048]{2,1,0:T(8,128)(2,1)} %copy.29, bf16[3,1,2048]{2,1,0:T(2,128)(2,1)S(1)} %collective-permute-done.3, bf16[3,1,2048]{2,1,0:T(2,128)(2,1)S(1)} %collective-permute-done.2, f32[512]{0:T(512)S(1)} %copy-done.6), kind=kLoop, calls=%fused_computation.1 | loop fusion | flops 34603008 | bytes 12609536 | tf_op jit(solution)/shard_map/convert_element_type | solution.py:42
  266.5 2.8 fusion.13
  269.3 3.1 fusion.6
  272.5 5.1 %convolution_bitcast_fusion = f32[3,64,2048]{2,1,0:T(8,128)} fusion(bf16[3,512,2048]{2,1,0:T(8,128)(2,1)} %copy-done.1, bf16[64,512]{1,0:T(8,128)(2,1)S(1)} %copy-done.5), kind=kOutput, calls=%fused_computation.11 | convolution fusion | flops 402653184 | bytes 7929856 | tf_op jit(solution)/shard_map/lc,bct->blt/dot_general | solution.py:46
  277.6 36.1 %all-reduce.8.cloned.1.call-done = (f32[3,512,64]{1,2,0:T(8,128)}, f32[3,512,128]{1,2,0:T(8,128)}) async-done(((f32[3,512,64]{1,2,0:T(8,128)}, f32[3,512,128]{1,2,0:T(8,128)}), (f32[3,512,64]{1,2,0:T(8,128)}, f32[3,512,128]{1,2,0:T(8,128)})) %all-reduce.8.cloned.1.call-update) | async-done | bytes 1179664 | tf_op jit(solution)/shard_map/psum | solution.py:53
  313.7 2.3 convolution_bitcast_fusion.1
  316.0 95.8 %all-reduce.6.cloned.1.call-done = (f32[3,64,2048]{2,1,0:T(8,128)}, f32[3,128,128]{1,2,0:T(8,128)}) async-done(((f32[3,64,2048]{2,1,0:T(8,128)}, f32[3,128,128]{1,2,0:T(8,128)}), (f32[3,64,2048]{2,1,0:T(8,128)}, f32[3,128,128]{1,2,0:T(8,128)})) %all-reduce.6.cloned.1.call-update) | async-done | bytes 1769488 | tf_op jit(solution)/shard_map/psum | solution.py:54
  411.8 1.7 copy.32
  413.6 1.8 copy.38
  415.3 2.7 copy.39
  (28 shorter events, 5.6 us)
Async XLA Ops:
  7.2 262.1 %copy-start = (bf16[2048,128]{1,0:T(8,128)(2,1)S(1)}, bf16[2048,128]{1,0:T(8,128)(2,1)}, u32[]{:S(2)}) copy-start(bf16[2048,128]{1,0:T(8,128)(2,1)} %param.13) | copy-start | bytes 1572868
  7.2 306.5 %all-reduce.8.cloned.1.call-start = ((), (), s32[]{:S(2)}) async-start(), calls=%async_computation.1 | async-start | bytes 2359296 | tf_op jit(solution)/shard_map/psum | solution.py:53
  10.9 191.5 %collective-permute-start = (bf16[512,127]{0,1:T(8,128)(2,1)}, bf16[512,127]{0,1:T(8,128)(2,1)S(1)}, u32[]{:S(2)}, u32[]{:S(2)}) collective-permute-start(bf16[512,127]{0,1:T(8,128)(2,1)} %get-tuple-element.21), channel_id=1, source_target_pairs={{0,1},{1,2},{2,3},{4,5},{5,6},{6,7},{8,9},{9,10},{10,11},{12,13},{... | collective-permute-start | bytes 390152 | tf_op jit(solution)/shard_map/ppermute | solution.py:12
  13.2 189.1 %collective-permute-start.1 = (bf16[512,127]{0,1:T(8,128)(2,1)}, bf16[512,127]{0,1:T(8,128)(2,1)S(1)}, u32[]{:S(2)}, u32[]{:S(2)}) collective-permute-start(bf16[512,127]{0,1:T(8,128)(2,1)} %get-tuple-element.20), channel_id=1, source_target_pairs={{1,0},{2,1},{3,2},{5,4},{6,5},{7,6},{9,8},{10,9},{11,10},{13,12},{... | collective-permute-start | bytes 390152 | tf_op jit(solution)/shard_map/ppermute | solution.py:15
  223.2 8.0 %copy-start.2 = (bf16[512,16,128]{2,0,1:T(8,128)(2,1)S(1)}, bf16[512,16,128]{2,0,1:T(8,128)(2,1)}, u32[]{:S(2)}) copy-start(bf16[512,16,128]{2,0,1:T(8,128)(2,1)} %copy.27) | copy-start | bytes 6291460
  238.1 20.1 %copy-start.6 = (f32[512]{0:T(512)S(1)}, f32[512]{0:T(512)}, u32[]{:S(2)}) copy-start(f32[512]{0:T(512)} %param.9) | copy-start | bytes 6148
  248.0 5.8 %collective-permute-start.3 = (bf16[3,1,2048]{2,1,0:T(2,128)(2,1)S(1)}, bf16[3,1,2048]{2,1,0:T(2,128)(2,1)S(1)}, u32[]{:S(2)}, u32[]{:S(2)}) collective-permute-start(bf16[3,1,2048]{2,1,0:T(2,128)(2,1)S(1)} %get-tuple-element.17), channel_id=1, source_target_pairs={{0,4},{4,8},{8,12},{12,16},{16,20},{20,24},{24,28},{1,5},{5,9},{9,... | collective-permute-start | bytes 36872 | tf_op jit(solution)/shard_map/ppermute | solution.py:12
  252.3 14.1 %copy-start.3 = (bf16[2048,64]{0,1:T(8,128)(2,1)S(1)}, bf16[2048,64]{0,1:T(8,128)(2,1)}, u32[]{:S(2)}) copy-start(bf16[2048,64]{0,1:T(8,128)(2,1)} %param.10) | copy-start | bytes 786436
  252.3 5.9 %collective-permute-start.2 = (bf16[3,1,2048]{2,1,0:T(2,128)(2,1)S(1)}, bf16[3,1,2048]{2,1,0:T(2,128)(2,1)S(1)}, u32[]{:S(2)}, u32[]{:S(2)}) collective-permute-start(bf16[3,1,2048]{2,1,0:T(2,128)(2,1)S(1)} %get-tuple-element.16), channel_id=1, source_target_pairs={{4,0},{8,4},{12,8},{16,12},{20,16},{24,20},{28,24},{5,1},{9,5},{13... | collective-permute-start | bytes 36872 | tf_op jit(solution)/shard_map/ppermute | solution.py:15
  266.4 2.8 copy-start.1
  266.4 6.0 %copy-start.5 = (bf16[64,512]{1,0:T(8,128)(2,1)S(1)}, bf16[64,512]{1,0:T(8,128)(2,1)}, u32[]{:S(2)}) copy-start(bf16[64,512]{1,0:T(8,128)(2,1)} %param.11) | copy-start | bytes 196612
  272.4 41.3 %copy-start.4 = (bf16[128,512]{1,0:T(8,128)(2,1)S(1)}, bf16[128,512]{1,0:T(8,128)(2,1)}, u32[]{:S(2)}) copy-start(bf16[128,512]{1,0:T(8,128)(2,1)} %param.12) | copy-start | bytes 393220
  272.4 139.4 %all-reduce.6.cloned.1.call-start = ((), (), s32[]{:S(2)}) async-start(), calls=%async_computation | async-start | bytes 3538944 | tf_op jit(solution)/shard_map/psum | solution.py:54
Sparse Core Ops, SparseCore 0:
  272.5 41.1 all-reduce.7
  317.9 93.9 all-reduce.5
where the time goes:
time: 427 us; the launch traced here: 425 us
  local copies, waits for them, and re-layouts  234 us (55%)
  waiting for transfers between devices  136 us (32%)
  matrix products  20.3 us (5%)
  between operations  14.2 us (3%)
  other arithmetic  10.9 us (3%)
  starting transfers between devices  9.4 us (2%)
    gather x2, local copies, waits for them, and re-layouts, on_device(): picked = jnp.take(band_taps, jnp.clip(offset, 0, tap_count - 1), axis=1)  187 us
    psum x1, waiting for transfers between devices, on_device(): corange_sketch = lax.psum(corange_part, 'chan')  95.8 us
    psum x1, waiting for transfers between devices, on_device(): range_sketch, projected_sum = lax.psum((range_part, projected), 'tm')  36.1 us
    concatenate x1, local copies, waits for them, and re-layouts, padded_2(): block = jnp.concatenate([low, block, high], axis=dim)  11.3 us
    unnamed x19, local copies, waits for them, and re-layouts  9.98 us
    convert_element_type x1, local copies, waits for them, and re-layouts, on_device(): filtered.reshape(band_count, channels, samples).astype(jnp.bfloat16)  8.93 us
  transfers between devices with their start and end apart: 6, of which 4 were waited for; matrix products, arithmetic and copies ran while one was open for 45% of the time, Pallas kernels for 0%

commit v1 on v0

v1 whole, which is shorter than its diff:
```python
import jax
import jax.numpy as jnp
from jax import lax
from jax.experimental import pallas as pl
from jax.experimental.pallas import tpu as pltpu
from jax.sharding import PartitionSpec as P

WIDE = 256
EDGE = 128
RIM = 16
F32 = jnp.float32
BF16 = jnp.bfloat16


def dot(a, b):
    return jnp.dot(a, b, preferred_element_type=F32)


def neighbours(low_part, high_part, axis):
    count = lax.axis_size(axis)
    forward = [(i, i + 1) for i in range(count - 1)]
    backward = [(target, source) for source, target in forward]
    return lax.ppermute(high_part, axis, forward), lax.ppermute(low_part, axis, backward)


def main_kernel(
    rec, left, right, low, high, vec, gain, rtest, ctest, weight, left_test,
    strain, rpart, core, ypart, toep_out,
    padded, toep, right_test, total,
):
    step = pl.program_id(0)
    rows, samples = rec.shape
    bands = vec.shape[0]
    own = pl.ds(RIM, rows)

    @pl.when(step == 0)
    def _():
        padded[own, EDGE : EDGE + samples] = rec[...]
        padded[own, 0:EDGE] = left[...]
        padded[own, EDGE + samples :] = right[...]
        padded[0:RIM, :] = low[...]
        padded[RIM + rows :, :] = high[...]
        for b in range(bands):
            spread = jnp.broadcast_to(vec[b : b + 1, :], (2 * WIDE, 2 * WIDE))
            skewed = pltpu.roll(spread, 0, 1, stride=1, stride_axis=0)
            toep[b] = skewed[:, :WIDE].astype(BF16)
        toep_out[...] = toep[...]
        right_test[:, 0:128] = ctest[...]
        right_test[:, 128:192] = rtest[...]
        right_test[:, 192:256] = jnp.zeros_like(rtest)
        both = dot(weight[...], padded[...])
        half = both.shape[0] // 2
        ypart[...] = both[:half] + both[half:]
        total[...] = jnp.zeros_like(total)

    start = pl.multiple_of(step * WIDE, WIDE)
    window = padded[:, pl.ds(start, 2 * WIDE)]
    test = right_test[pl.ds(start, WIDE), :]
    for b in range(bands):
        filtered = dot(window, toep[b]).astype(BF16).astype(F32)
        after = pltpu.roll(filtered, filtered.shape[0] - 1, 0)
        before = pltpu.roll(filtered, 1, 0)
        value = (gain[...] * (after - before)[RIM : RIM + rows]).astype(BF16)
        strain[b] = value
        total[b] += dot(value, test)

    @pl.when(step == pl.num_programs(0) - 1)
    def _():
        for b in range(bands):
            rpart[b] = total[b, :, 128:192]
            projected = total[b, :, 0:128]
            top = projected.astype(BF16)
            rest = (projected - top.astype(F32)).astype(BF16)
            core[b] = dot(left_test[...], top) + dot(left_test[...], rest)


def corange_kernel(ysum, toep, out):
    step = pl.program_id(0)
    start = pl.multiple_of(step * WIDE, WIDE)
    window = ysum[:, pl.ds(start, 2 * WIDE)].astype(BF16)
    for b in range(out.shape[0]):
        out[b] = dot(window, toep[b])


def whole(shape):
    return pl.BlockSpec(shape, lambda *_: (0,) * len(shape))


def on_device(recording, band_taps, channel_gain, range_test, corange_test, core_left, core_right):
    rows, samples = recording.shape
    bands, taps = band_taps.shape
    steps = samples // WIDE
    span = samples + 2 * EDGE
    left, right = neighbours(recording[:, :EDGE], recording[:, -EDGE:], "tm")
    first = jnp.concatenate([left[:1], recording[:1], right[:1]], axis=1)
    last = jnp.concatenate([left[-1:], recording[-1:], right[-1:]], axis=1)
    below, above = neighbours(first, last, "chan")
    low = jnp.pad(below, ((RIM - 1, 0), (0, 0)))
    high = jnp.pad(above, ((0, RIM - 1), (0, 0)))
    vec = jnp.pad(band_taps[:, ::-1].astype(F32), ((0, 0), (2 * WIDE - taps, 0)))
    scaled = corange_test.astype(F32) * channel_gain[None, :]
    weight = jnp.pad(scaled, ((0, 0), (RIM + 1, RIM - 1))) - jnp.pad(
        scaled, ((0, 0), (RIM - 1, RIM + 1))
    )
    top = weight.astype(BF16)
    rest = (weight - top.astype(F32)).astype(BF16)
    weight = jnp.concatenate([top, rest], axis=0)
    operands = (
        recording, left, right, low, high, vec, channel_gain[:, None],
        range_test, core_right, weight, core_left,
    )
    rank, core_rank, corank = range_test.shape[1], core_left.shape[0], corange_test.shape[0]
    strain, rpart, core, ypart, toep = pl.pallas_call(
        main_kernel,
        grid=(steps,),
        in_specs=[whole(x.shape) for x in operands],
        out_specs=[
            pl.BlockSpec((bands, rows, WIDE), lambda j: (0, 0, j)),
            whole((bands, rows, rank)),
            whole((bands, core_rank, core_rank)),
            whole((corank, span)),
            whole((bands, 2 * WIDE, WIDE)),
        ],
        out_shape=[
            jax.ShapeDtypeStruct((bands, rows, samples), BF16),
            jax.ShapeDtypeStruct((bands, rows, rank), F32),
            jax.ShapeDtypeStruct((bands, core_rank, core_rank), F32),
            jax.ShapeDtypeStruct((corank, span), F32),
            jax.ShapeDtypeStruct((bands, 2 * WIDE, WIDE), BF16),
        ],
        scratch_shapes=[
            pltpu.VMEM((rows + 2 * RIM, span), BF16),
            pltpu.VMEM((bands, 2 * WIDE, WIDE), BF16),
            pltpu.VMEM((samples, 256), BF16),
            pltpu.VMEM((bands, rows, 256), F32),
        ],
        compiler_params=pltpu.CompilerParams(vmem_limit_bytes=48 * 2**20),
    )(*operands)
    ysum = lax.psum(ypart, "chan")
    range_sketch = lax.psum(rpart, "tm")
    core_sketch = lax.psum(core, ("chan", "tm"))
    corange_sketch = pl.pallas_call(
        corange_kernel,
        grid=(steps,),
        in_specs=[whole(ysum.shape), whole(toep.shape)],
        out_specs=pl.BlockSpec((bands, corank, WIDE), lambda j: (0, 0, j)),
        out_shape=jax.ShapeDtypeStruct((bands, corank, samples), F32),
    )(ysum, toep)
    return strain, range_sketch, corange_sketch, core_sketch


def solution(mesh):
    in_specs = (
        P("chan", "tm"),
        P(),
        P("chan"),
        P("tm", None),
        P(None, "chan"),
        P(None, "chan"),
        P("tm", None),
    )
    out_specs = (P(None, "chan", "tm"), P(None, "chan", None), P(None, None, "tm"), P())
    return jax.shard_map(
        on_device, mesh=mesh, in_specs=in_specs, out_specs=out_specs, check_vma=False
    )
```

time: 427 us -> 294 us (0.69)
  local copies, waits for them, and re-layouts: 234 us -> 9.52 us
  waiting for transfers between devices: 136 us -> 237 us
  Pallas kernels: 0 us -> 21.1 us
  matrix products: 20.3 us -> 0 us
  other arithmetic: 10.9 us -> 1.13 us
    gather x2 -> x0, local copies, waits for them, and re-layouts: 187 us -> none  [on_device(): picked = jnp.take(band_taps, jnp.clip(offset, 0, tap_count - 1), axis=1)]
    psum x2 -> x3, waiting for transfers between devices: 132 us -> 233 us  [the longest x1 124 us: on_device(): core_sketch = lax.psum(core, ('chan', 'tm'))]
    pallas_call x0 -> x2, Pallas kernels: none -> 21.1 us  [the longest x1 15.8 us: on_device(): pl.pallas_call(main_kernel, grid=(steps,), in_specs=[whole(x.shape) for x...]
    dot_general x5 -> x0, matrix products: 20.3 us -> none  [the longest x1 6.91 us: on_device(): jnp.einsum('cnw,bwo->bcno', windows, toeplitz, preferred_element_type=jnp...]
    reshape x3 -> x0, local copies, waits for them, and re-layouts: 11.9 us -> none  [the longest x1 4.06 us: on_device(): mid_block = padded[:, 128:samples + 128].reshape(channels, blocks, 128)]
    concatenate x1 -> x0, local copies, waits for them, and re-layouts: 11.3 us -> none  [padded_2(): block = jnp.concatenate([low, block, high], axis=dim)]
    convert_element_type x1 -> x0, local copies, waits for them, and re-layouts: 8.93 us -> none  [on_device(): filtered.reshape(band_count, channels, samples).astype(jnp.bfloat16)]
    convert_element_type x1, other arithmetic: 8.26 us -> 0.15 us  [on_device(): top = weight.astype(BF16)]
  transfers between devices with their start and end apart: 6 -> 7, of which waited for: 4 -> 4; matrix products, arithmetic and copies ran while one was open for 45% -> 2% of each run, Pallas kernels for 0% -> 2%
where the time goes in v1:
time: 294 us; the launch traced here: 293 us
  waiting for transfers between devices  237 us (81%)
  Pallas kernels  21.1 us (7%)
  between operations  13.9 us (5%)
  starting transfers between devices  10.6 us (4%)
  local copies, waits for them, and re-layouts  9.52 us (3%)
    psum x1, waiting for transfers between devices, on_device(): core_sketch = lax.psum(core, ('chan', 'tm'))  124 us
    psum x1, waiting for transfers between devices, on_device(): ysum = lax.psum(ypart, 'chan')  74.3 us
    psum x1, waiting for transfers between devices, on_device(): range_sketch = lax.psum(rpart, 'tm')  35.5 us
    pallas_call x1, Pallas kernels, on_device(): pl.pallas_call(main_kernel, grid=(steps,), in_specs=[whole(x.shape) for x...  15.8 us
    ppermute x2, starting transfers between devices, neighbours(): lax.ppermute(high_part, axis, forward)  7.91 us
    unnamed x11, local copies, waits for them, and re-layouts  6.82 us
  transfers between devices with their start and end apart: 7, of which 4 were waited for; matrix products, arithmetic and copies ran while one was open for 2% of the time, Pallas kernels for 2%

profile of v1, /device:TPU:0, one launch (start us, length us, event | category | flops | bytes accessed | tf_op | source)
XLA Modules:
  0.0 293.2 jit_solution(18114079993285190591)
XLA Ops:
  7.2 1.0 fusion.2
  8.3 1.3 collective-permute-start.1
  9.6 3.0 %collective-permute-start = (bf16[512,128]{1,0:T(8,128)(2,1)S(1)}, bf16[512,128]{1,0:T(8,128)(2,1)S(1)}, u32[]{:S(2)}, u32[]{:S(2)}) collective-permute-start(bf16[512,128]{1,0:T(8,128)(2,1)S(1)} %get-tuple-element.25), channel_id=1, source_target_pairs={{0,1},{1,2},{2,3},{4,5},{5,6},{6,7},{8,9},{9,10},{10,11},{12,13},{... | collective-permute-start | bytes 393224 | tf_op jit(solution)/shard_map/ppermute | solution.py:23
  12.6 0.8 fusion.1
  13.4 0.9 convert_multiply_fusion
  14.3 0.2 fusion
  14.4 0.9 reverse
  15.3 0.1 slice.36
  15.5 4.9 %collective-permute-start.2 = (bf16[1,2304]{1,0:T(2,128)(2,1)S(1)}, bf16[1,2304]{1,0:T(2,128)(2,1)S(1)}, u32[]{:S(2)}, u32[]{:S(2)}) collective-permute-start(bf16[1,2304]{1,0:T(2,128)(2,1)S(1)} %pad_maximum_fusion.1), channel_id=1, source_target_pairs={{0,4},{4,8},{8,12},{12,16},{16,20},{20,24},{24,28},{1,5},{5,9},{9,... | collective-permute-start | bytes 13832 | tf_op jit(solution)/shard_map/ppermute | solution.py:23
  20.4 1.3 collective-permute-start.3
  21.7 0.1 pad_convert_fusion.vec
  21.7 0.8 copy.13.gain
  22.6 1.2 copy.14.rtest
  23.8 2.1 collective-permute-done.3
  26.0 15.8 %shard_map.102 = (bf16[3,512,2048]{2,1,0:T(8,128)(2,1)}, f32[3,512,64]{2,1,0:T(8,128)}, f32[3,128,128]{2,1,0:T(8,128)}, f32[64,2304]{1,0:T(8,128)}, bf16[3,512,256]{2,1,0:T(8,128)(2,1)S(1)}) custom-call(bf16[512,2048]{1,0:T(8,128)(2,1)} %rec.1, bf16[512,128]{1,0:T(8,128)(2,1)S(1)} %collective-permute-done.left, ...), custom_call_target="tpu_custom_call" | custom-call | tf_op jit(solution)/shard_map/pallas_call | solution.py:113
  41.8 0.9 copy-done
  42.8 0.7 all-reduce.11.cloned.1.call-update
  43.5 0.7 all-reduce.13.cloned.1.call-update
  44.2 35.5 %all-reduce.9.cloned.1.call-done = f32[3,512,64]{2,1,0:T(8,128)} async-done(((f32[3,512,64]{2,1,0:T(8,128)}), f32[3,512,64]{2,1,0:T(8,128)}) %all-reduce.9.cloned.1.call-update) | async-done | bytes 393232 | tf_op jit(solution)/shard_map/psum | solution.py:140
  79.7 2.1 copy.15
  81.8 74.3 %all-reduce.11.cloned.1.call-done.ysum = f32[64,2304]{1,0:T(8,128)} async-done(((f32[64,2304]{1,0:T(8,128)}), f32[64,2304]{1,0:T(8,128)}) %all-reduce.11.cloned.1.call-update) | async-done | bytes 589840 | tf_op jit(solution)/shard_map/psum | solution.py:139
  156.1 5.3 %shard_map.103 = f32[3,64,2048]{2,1,0:T(8,128)} custom-call(f32[64,2304]{1,0:T(8,128)} %all-reduce.11.cloned.1.call-done.ysum, bf16[3,512,256]{2,1,0:T(8,128)(2,1)} %copy-done), custom_call_target="tpu_custom_call" | custom-call | tf_op jit(solution)/shard_map/pallas_call | solution.py:142
  161.4 123.7 %all-reduce.13.cloned.1.call-done = f32[3,128,128]{2,1,0:T(8,128)} async-done(((f32[3,128,128]{2,1,0:T(8,128)}), f32[3,128,128]{2,1,0:T(8,128)}) %all-reduce.13.cloned.1.call-update) | async-done | bytes 196624 | tf_op jit(solution)/shard_map/psum | solution.py:141
  285.1 1.6 copy.19
  (19 shorter events, 0.2 us)
Async XLA Ops:
  7.2 18.8 %copy-start.1 = (bf16[2048,128]{1,0:T(8,128)(2,1)S(1)}, bf16[2048,128]{1,0:T(8,128)(2,1)}, u32[]{:S(2)}) copy-start(bf16[2048,128]{1,0:T(8,128)(2,1)} %ctest.1) | copy-start | bytes 1572868
  7.2 18.8 %copy-start.2 = (bf16[128,512]{1,0:T(8,128)(2,1)S(1)}, bf16[128,512]{1,0:T(8,128)(2,1)}, u32[]{:S(2)}) copy-start(bf16[128,512]{1,0:T(8,128)(2,1)} %left_test.1) | copy-start | bytes 393220
  7.2 72.5 %all-reduce.9.cloned.1.call-start = ((), (), s32[]{:S(2)}) async-start(), calls=%async_computation | async-start | bytes 1572864 | tf_op jit(solution)/shard_map/psum | solution.py:140
  8.3 7.1 %collective-permute-start.1 = (bf16[512,128]{1,0:T(8,128)(2,1)S(1)}, bf16[512,128]{1,0:T(8,128)(2,1)S(1)}, u32[]{:S(2)}, u32[]{:S(2)}) collective-permute-start(bf16[512,128]{1,0:T(8,128)(2,1)S(1)} %get-tuple-element.24), channel_id=1, source_target_pairs={{1,0},{2,1},{3,2},{5,4},{6,5},{7,6},{9,8},{10,9},{11,10},{13,12},{... | collective-permute-start | bytes 393224 | tf_op jit(solution)/shard_map/ppermute | solution.py:23
  9.6 5.8 %collective-permute-start = (bf16[512,128]{1,0:T(8,128)(2,1)S(1)}, bf16[512,128]{1,0:T(8,128)(2,1)S(1)}, u32[]{:S(2)}, u32[]{:S(2)}) collective-permute-start(bf16[512,128]{1,0:T(8,128)(2,1)S(1)} %get-tuple-element.25), channel_id=1, source_target_pairs={{0,1},{1,2},{2,3},{4,5},{5,6},{6,7},{8,9},{9,10},{10,11},{12,13},{... | collective-permute-start | bytes 393224 | tf_op jit(solution)/shard_map/ppermute | solution.py:23
  15.5 10.5 %collective-permute-start.2 = (bf16[1,2304]{1,0:T(2,128)(2,1)S(1)}, bf16[1,2304]{1,0:T(2,128)(2,1)S(1)}, u32[]{:S(2)}, u32[]{:S(2)}) collective-permute-start(bf16[1,2304]{1,0:T(2,128)(2,1)S(1)} %pad_maximum_fusion.1), channel_id=1, source_target_pairs={{0,4},{4,8},{8,12},{12,16},{16,20},{20,24},{24,28},{1,5},{5,9},{9,... | collective-permute-start | bytes 13832 | tf_op jit(solution)/shard_map/ppermute | solution.py:23
  20.4 5.6 %collective-permute-start.3 = (bf16[1,2304]{1,0:T(2,128)(2,1)S(1)}, bf16[1,2304]{1,0:T(2,128)(2,1)S(1)}, u32[]{:S(2)}, u32[]{:S(2)}) collective-permute-start(bf16[1,2304]{1,0:T(2,128)(2,1)S(1)} %pad_maximum_fusion.2), channel_id=1, source_target_pairs={{4,0},{8,4},{12,8},{16,12},{20,16},{24,20},{28,24},{5,1},{9,5},{13... | collective-permute-start | bytes 13832 | tf_op jit(solution)/shard_map/ppermute | solution.py:23
  41.8 0.9 copy-start
  42.7 113.4 %all-reduce.11.cloned.1.call-start = ((), (), s32[]{:S(2)}) async-start(), calls=%async_computation.1 | async-start | bytes 1179648 | tf_op jit(solution)/shard_map/psum | solution.py:139
  43.5 241.6 %all-reduce.13.cloned.1.call-start = ((), (), s32[]{:S(2)}) async-start(), calls=%async_computation.2 | async-start | bytes 393216 | tf_op jit(solution)/shard_map/psum | solution.py:141
Sparse Core Ops, SparseCore 0:
  42.8 36.7 all-reduce.8
  83.0 72.9 all-reduce.10
  163.1 121.9 all-reduce.12

commit v2 on v1

--- a/solution.py
+++ b/solution.py
@@ -67,19 +67,134 @@
     @pl.when(step == pl.num_programs(0) - 1)
     def _():
         for b in range(bands):
-            rpart[b] = total[b, :, 128:192]
+            for c in range(rows // 128):
+                turned = total[b, c * 128 : (c + 1) * 128, 128:256].T
+                at = (c * bands + b) * rtest.shape[1]
+                rpart[at : at + rtest.shape[1], :] = turned[: rtest.shape[1]]
             projected = total[b, :, 0:128]
             top = projected.astype(BF16)
             rest = (projected - top.astype(F32)).astype(BF16)
-            core[b] = dot(left_test[...], top) + dot(left_test[...], rest)
-
-
-def corange_kernel(ysum, toep, out):
-    step = pl.program_id(0)
-    start = pl.multiple_of(step * WIDE, WIDE)
-    window = ysum[:, pl.ds(start, 2 * WIDE)].astype(BF16)
-    for b in range(out.shape[0]):
-        out[b] = dot(window, toep[b])
+            core[b * 128 : (b + 1) * 128, :] = dot(left_test[...], top) + dot(left_test[...], rest)
+
+
+def share_kernel(
+    rpart, core, ypart, toep, rout, yout, cout,
+    tm_send, tm_recv, rall, csend, call, y_send, y_recv, yall, yfull,
+    tm_sems, r_sems, c_sems, call_sems, y_sems, yall_sems,
+):
+    times, blocks = rall.shape[0], yall.shape[0]
+    here_t, here_c = lax.axis_index("tm"), lax.axis_index("chan")
+    bands, rank, rows = rout.shape
+    nr, nc = rall.shape[1], call.shape[1]
+    span = ypart.shape[1]
+    piece, width = ypart.shape[0] // blocks, yall.shape[2]
+
+    def peer(axis, d):
+        if axis == "tm":
+            return lax.rem(here_t + d, times)
+        return lax.rem(here_c + d, blocks)
+
+    def send(src, dst, sems, axis, d):
+        copy = pltpu.make_async_remote_copy(
+            src_ref=src, dst_ref=dst, send_sem=sems.at[0, d - 1], recv_sem=sems.at[1, d - 1],
+            device_id={axis: peer(axis, d)}, device_id_type=pl.DeviceIdType.MESH,
+        )
+        copy.start()
+        return copy
+
+    barrier = pltpu.get_barrier_semaphore()
+    for axis, count in (("tm", times), ("chan", blocks)):
+        for d in range(1, count):
+            pl.semaphore_signal(
+                barrier, inc=1, device_id={axis: peer(axis, d)},
+                device_id_type=pl.DeviceIdType.MESH,
+            )
+    for p in range(blocks):
+        block = ypart[p * piece : (p + 1) * piece, :]
+        if width < span:
+            block = jnp.concatenate(
+                [block[:, k : k + width] for k in range(0, span, width)], axis=0
+            )
+        elif piece < RIM:
+            block = jnp.concatenate([block, jnp.zeros((RIM - piece, span), F32)], axis=0)
+        y_send[p] = block.astype(BF16)
+    for q in range(times):
+        tm_send[q, 0:nr] = rpart[q * nr : (q + 1) * nr, :].astype(BF16)
+        tm_send[q, nr : nr + nc] = core[q * nc : (q + 1) * nc, :].astype(BF16)
+    pl.semaphore_wait(barrier, times + blocks - 2)
+
+    tm_copies = [
+        send(tm_send.at[peer("tm", d)], tm_recv.at[d - 1], tm_sems, "tm", d)
+        for d in range(1, times)
+    ]
+    y_copies = [
+        send(y_send.at[peer("chan", d)], y_recv.at[d - 1], y_sems, "chan", d)
+        for d in range(1, blocks)
+    ]
+    summed = tm_send[here_t].astype(F32)
+    for d in range(1, times):
+        tm_copies[d - 1].wait_recv()
+        summed += tm_recv[d - 1].astype(F32)
+    rall[here_t] = summed[0:nr].astype(BF16)
+    call[here_c] = summed[nr : nr + nc].astype(BF16)
+    c_copies = [
+        send(call.at[here_c], call.at[here_c], call_sems, "chan", d) for d in range(1, blocks)
+    ]
+    r_copies = [send(rall.at[here_t], rall.at[here_t], r_sems, "tm", d) for d in range(1, times)]
+
+    y_sum = y_send[here_c].astype(F32)
+    for d in range(1, blocks):
+        y_copies[d - 1].wait_recv()
+        y_sum += y_recv[d - 1].astype(F32)
+    yall[here_c] = y_sum.astype(BF16)
+    yall_copies = [
+        send(yall.at[here_c], yall.at[here_c], yall_sems, "chan", d) for d in range(1, blocks)
+    ]
+
+    for copy in c_copies:
+        copy.wait_recv()
+    c_sum = call[0].astype(F32)
+    for p in range(1, blocks):
+        c_sum += call[p].astype(F32)
+    csend[here_t] = c_sum
+    core_copies = [
+        send(csend.at[here_t], csend.at[here_t], c_sems, "tm", d) for d in range(1, times)
+    ]
+
+    for copy in r_copies:
+        copy.wait_recv()
+    per = nr // RIM
+    for c in range(rows // 128):
+        for b in range(bands):
+            for k in range(rank // RIM):
+                at = ((c * bands + b) * rank) // RIM + k
+                part = rall[at // per, (at % per) * RIM : (at % per + 1) * RIM, :]
+                rout[b, k * RIM : (k + 1) * RIM, c * 128 : (c + 1) * 128] = part.astype(F32)
+
+    for copy in yall_copies:
+        copy.wait_recv()
+    for p in range(blocks):
+        block = yall[p].astype(F32)[: piece * (span // width)]
+        if width < span:
+            block = jnp.concatenate(
+                [block[k * piece : (k + 1) * piece] for k in range(span // width)], axis=1
+            )
+        yfull[p * piece : (p + 1) * piece, :] = block
+    corank, samples = yout.shape[1:]
+    window = jnp.concatenate(
+        [yfull[:, k : k + 2 * WIDE].astype(BF16) for k in range(0, samples, WIDE)], axis=0
+    )
+    for b in range(bands):
+        result = dot(window, toep[b])
+        for k in range(samples // WIDE):
+            yout[b, :, k * WIDE : (k + 1) * WIDE] = result[k * corank : (k + 1) * corank]
+
+    for copy in core_copies:
+        copy.wait_recv()
+    for q in range(times):
+        cout[q * nc : (q + 1) * nc, :] = csend[q]
+    for copy in tm_copies + y_copies + c_copies + r_copies + yall_copies + core_copies:
+        copy.wait_send()
 
 
 def whole(shape):
@@ -116,15 +231,15 @@
         in_specs=[whole(x.shape) for x in operands],
         out_specs=[
             pl.BlockSpec((bands, rows, WIDE), lambda j: (0, 0, j)),
-            whole((bands, rows, rank)),
-            whole((bands, core_rank, core_rank)),
+            whole((bands * rank * rows // 128, 128)),
+            whole((bands * core_rank, core_rank)),
             whole((corank, span)),
             whole((bands, 2 * WIDE, WIDE)),
         ],
         out_shape=[
             jax.ShapeDtypeStruct((bands, rows, samples), BF16),
-            jax.ShapeDtypeStruct((bands, rows, rank), F32),
-            jax.ShapeDtypeStruct((bands, core_rank, core_rank), F32),
+            jax.ShapeDtypeStruct((bands * rank * rows // 128, 128), F32),
+            jax.ShapeDtypeStruct((bands * core_rank, core_rank), F32),
             jax.ShapeDtypeStruct((corank, span), F32),
             jax.ShapeDtypeStruct((bands, 2 * WIDE, WIDE), BF16),
         ],
@@ -136,16 +251,45 @@
         ],
         compiler_params=pltpu.CompilerParams(vmem_limit_bytes=48 * 2**20),
     )(*operands)
-    ysum = lax.psum(ypart, "chan")
-    range_sketch = lax.psum(rpart, "tm")
-    core_sketch = lax.psum(core, ("chan", "tm"))
-    corange_sketch = pl.pallas_call(
-        corange_kernel,
-        grid=(steps,),
-        in_specs=[whole(ysum.shape), whole(toep.shape)],
-        out_specs=pl.BlockSpec((bands, corank, WIDE), lambda j: (0, 0, j)),
-        out_shape=jax.ShapeDtypeStruct((bands, corank, samples), F32),
-    )(ysum, toep)
+    times, blocks = lax.axis_size("tm"), lax.axis_size("chan")
+    nr, nc = rpart.shape[0] // times, core.shape[0] // times
+    piece = corank // blocks
+    fold = max(1, RIM // piece)
+    if span % (fold * 128):
+        fold = 1
+    tile = (max(RIM, piece), span // fold)
+    vmem = pl.BlockSpec(memory_space=pltpu.VMEM)
+
+    def sems(count):
+        return pltpu.SemaphoreType.DMA((2, count - 1))
+
+    ranges, corange_sketch, core_sketch = pl.pallas_call(
+        share_kernel,
+        in_specs=[vmem] * 4,
+        out_specs=[vmem] * 3,
+        out_shape=[
+            jax.ShapeDtypeStruct((bands, rank, rows), F32),
+            jax.ShapeDtypeStruct((bands, corank, samples), F32),
+            jax.ShapeDtypeStruct((bands * core_rank, core_rank), F32),
+        ],
+        scratch_shapes=[
+            pltpu.VMEM((times, nr + nc, 128), BF16),
+            pltpu.VMEM((times - 1, nr + nc, 128), BF16),
+            pltpu.VMEM((times, nr, 128), BF16),
+            pltpu.VMEM((times, nc, 128), F32),
+            pltpu.VMEM((blocks, nc, 128), BF16),
+            pltpu.VMEM((blocks,) + tile, BF16),
+            pltpu.VMEM((blocks - 1,) + tile, BF16),
+            pltpu.VMEM((blocks,) + tile, BF16),
+            pltpu.VMEM((corank, span), F32),
+            sems(times), sems(times), sems(times), sems(blocks), sems(blocks), sems(blocks),
+        ],
+        compiler_params=pltpu.CompilerParams(
+            collective_id=0, has_side_effects=True, vmem_limit_bytes=40 * 2**20
+        ),
+    )(rpart, core, ypart, toep)
+    range_sketch = jnp.swapaxes(ranges, 1, 2)
+    core_sketch = core_sketch.reshape(bands, core_rank, core_rank)
     return strain, range_sketch, corange_sketch, core_sketch
 
 

time: 294 us -> 60 us (0.20)
  waiting for transfers between devices: 237 us -> 2.13 us
  Pallas kernels: 21.1 us -> 36.4 us
  between operations: 13.9 us -> 0.81 us
    psum x3 -> x0, waiting for transfers between devices: 233 us -> none  [the longest x1 124 us: on_device(): core_sketch = lax.psum(core, ('chan', 'tm'))]
    pallas_call x1, Pallas kernels: 5.34 us -> 22.9 us  [on_device(): pl.pallas_call(share_kernel, in_specs=[vmem] * 4, out_specs=[vmem] * 3, o...]
    unnamed x11 -> x12, local copies, waits for them, and re-layouts: 6.82 us -> 5.78 us
  transfers between devices with their start and end apart: 7 -> 4, of which waited for: 4 -> 1; matrix products, arithmetic and copies ran while one was open for 2% -> 8% of each run, Pallas kernels for 2% -> 0%
where the time goes in v2:
time: 60 us; the launch traced here: 59.5 us
  Pallas kernels  36.4 us (61%)
  starting transfers between devices  10.5 us (18%)
  local copies, waits for them, and re-layouts  8.58 us (14%)
  waiting for transfers between devices  2.13 us (4%)
  other arithmetic  1.13 us (2%)
  between operations  0.81 us (1%)
    pallas_call x1, Pallas kernels, on_device(): pl.pallas_call(share_kernel, in_specs=[vmem] * 4, out_specs=[vmem] * 3, o...  22.9 us
    pallas_call x1, Pallas kernels, on_device(): pl.pallas_call(main_kernel, grid=(steps,), in_specs=[whole(x.shape) for x...  13.5 us
    ppermute x2, starting transfers between devices, neighbours(): lax.ppermute(high_part, axis, forward)  7.91 us
    unnamed x12, local copies, waits for them, and re-layouts  5.78 us
    ppermute x2, starting transfers between devices, neighbours(): lax.ppermute(low_part, axis, backward)  2.58 us
    ppermute x2, waiting for transfers between devices, neighbours(): lax.ppermute(low_part, axis, backward)  2.12 us
  transfers between devices with their start and end apart: 4, of which 1 were waited for; matrix products, arithmetic and copies ran while one was open for 8% of the time, Pallas kernels for 0%

profile of v2, /device:TPU:0, one launch (start us, length us, event | category | flops | bytes accessed | tf_op | source)
XLA Modules:
  0.0 59.5 jit_solution(3306828167914799860)
XLA Ops:
  0.6 0.0 copy-start
  0.7 1.1 %fusion.2 = (bf16[512,128]{1,0:T(8,128)(2,1)S(1)}, bf16[512,128]{1,0:T(8,128)(2,1)S(1)}) fusion(bf16[512,2048]{1,0:T(8,128)(2,1)} %rec.1), kind=kLoop, calls=%fused_computation.9 | loop fusion | bytes 524288 | tf_op jit(solution)/shard_map/slice | solution.py:209
  1.8 1.3 %collective-permute-start.1 = (bf16[512,128]{1,0:T(8,128)(2,1)S(1)}, bf16[512,128]{1,0:T(8,128)(2,1)S(1)}, u32[]{:S(2)}, u32[]{:S(2)}) collective-permute-start(bf16[512,128]{1,0:T(8,128)(2,1)S(1)} %get-tuple-element.22), channel_id=1, source_target_pairs={{1,0},{2,1},{3,2},{5,4},{6,5},{7,6},{9,8},{10,9},{11,10},{13,12},{... | collective-permute-start | bytes 393224 | tf_op jit(solution)/shard_map/ppermute | solution.py:23
  3.1 3.0 %collective-permute-start = (bf16[512,128]{1,0:T(8,128)(2,1)S(1)}, bf16[512,128]{1,0:T(8,128)(2,1)S(1)}, u32[]{:S(2)}, u32[]{:S(2)}) collective-permute-start(bf16[512,128]{1,0:T(8,128)(2,1)S(1)} %get-tuple-element.23), channel_id=1, source_target_pairs={{0,1},{1,2},{2,3},{4,5},{5,6},{6,7},{8,9},{9,10},{10,11},{12,13},{... | collective-permute-start | bytes 393224 | tf_op jit(solution)/shard_map/ppermute | solution.py:23
  6.1 0.8 %fusion.1 = (bf16[1,2048]{1,0:T(2,128)(2,1)S(1)}, bf16[1,2048]{1,0:T(2,128)(2,1)S(1)}) fusion(bf16[512,2048]{1,0:T(8,128)(2,1)} %rec.1), kind=kLoop, calls=%fused_computation.8 | loop fusion | bytes 16384 | tf_op jit(solution)/shard_map/slice | solution.py:210
  6.9 0.9 %convert_multiply_fusion = f32[64,512]{1,0:T(8,128)S(1)} fusion(bf16[64,512]{1,0:T(8,128)(2,1)} %param.11, f32[512]{0:T(512)} %param.9), kind=kLoop, calls=%fused_computation.4 | loop fusion | flops 65536 | bytes 198656 | tf_op jit(solution)/shard_map/mul | solution.py:216
  7.8 0.2 fusion
  8.0 0.9 %reverse = bf16[3,256]{1,0:T(4,128)(2,1)S(1)} reverse(bf16[3,256]{1,0:T(4,128)(2,1)} %bitcast.7), dimensions={1} | reverse | bytes 3072
  8.8 0.1 slice.36
  8.9 0.0 collective-permute-done.1.right
  8.9 0.0 collective-permute-done.left
  9.0 4.9 %collective-permute-start.2 = (bf16[1,2304]{1,0:T(2,128)(2,1)S(1)}, bf16[1,2304]{1,0:T(2,128)(2,1)S(1)}, u32[]{:S(2)}, u32[]{:S(2)}) collective-permute-start(bf16[1,2304]{1,0:T(2,128)(2,1)S(1)} %pad_maximum_fusion.1), channel_id=1, source_target_pairs={{0,4},{4,8},{8,12},{12,16},{16,20},{20,24},{24,28},{1,5},{5,9},{9,... | collective-permute-start | bytes 13832 | tf_op jit(solution)/shard_map/ppermute | solution.py:23
  13.9 1.3 %collective-permute-start.3 = (bf16[1,2304]{1,0:T(2,128)(2,1)S(1)}, bf16[1,2304]{1,0:T(2,128)(2,1)S(1)}, u32[]{:S(2)}, u32[]{:S(2)}) collective-permute-start(bf16[1,2304]{1,0:T(2,128)(2,1)S(1)} %pad_maximum_fusion.2), channel_id=1, source_target_pairs={{4,0},{8,4},{12,8},{16,12},{20,16},{24,20},{28,24},{5,1},{9,5},{13... | collective-permute-start | bytes 13832 | tf_op jit(solution)/shard_map/ppermute | solution.py:23
  15.2 0.1 pad_convert_fusion.vec
  15.3 0.8 %copy.12.gain = f32[512,1]{1,0:T(8,128)S(1)} copy(f32[512,1]{0,1:T(1,128)} %bitcast.6) | data formatting | bytes 4096 | tf_op jit(solution)/shard_map/broadcast_in_dim | solution.py:224
  16.1 1.2 %copy.13.rtest = bf16[2048,64]{1,0:T(8,128)(2,1)S(1)} copy(bf16[2048,64]{0,1:T(8,128)(2,1)} %param.10) | data formatting | bytes 524288 | tf_op args[3]
  17.3 2.1 %collective-permute-done.3 = bf16[1,2304]{1,0:T(2,128)(2,1)S(1)} collective-permute-done((bf16[1,2304]{1,0:T(2,128)(2,1)S(1)}, bf16[1,2304]{1,0:T(2,128)(2,1)S(1)}, u32[]{:S(2)}, u32[]{:S(2)}) %collective-permute-start.3) | collective-permute-done | bytes 4640 | tf_op jit(solution)/shard_map/ppermute | solution.py:23
  19.5 0.0 copy-start.1
  19.5 1.0 %copy-done.1 = bf16[2048,128]{1,0:T(8,128)(2,1)S(1)} copy-done((bf16[2048,128]{1,0:T(8,128)(2,1)S(1)}, bf16[2048,128]{1,0:T(8,128)(2,1)}, u32[]{:S(2)}) %copy-start.1) | copy-done | bytes 524312
  20.6 13.5 %shard_map.102 = (bf16[3,512,2048]{2,1,0:T(8,128)(2,1)}, f32[768,128]{1,0:T(8,128)S(1)}, f32[384,128]{1,0:T(8,128)S(1)}, f32[64,2304]{1,0:T(8,128)S(1)}, bf16[3,512,256]{2,1,0:T(8,128)(2,1)S(1)}) custom-call(bf16[512,2048]{1,0:T(8,128)(2,1)S(1)} %copy-done, bf16[512,128]{1,0:T(8,128)(2,1)S(1)} %collective-permute-done.left, ...), custom_call_target="tpu_custom_call" | custom-call | tf_op jit(solution)/shard_map/pallas_call | solution.py:228
  34.1 22.9 %shard_map.103 = (f32[3,64,512]{2,1,0:T(8,128)S(1)}, f32[3,64,2048]{2,1,0:T(8,128)S(1)}, f32[384,128]{1,0:T(8,128)S(1)}) custom-call(f32[768,128]{1,0:T(8,128)S(1)} %get-tuple-element.13.rpart, f32[384,128]{1,0:T(8,128)S(1)} %get-tuple-element.14.core, f32[64,2304]{1,0:T(8,128)S(1)} %get-tuple-element.15.ypart, bf16[3,512,256]{2,1,0:T(8,128)(2,1)S(1)} %get-tuple-element.16.toep), custom_call_target="tpu_custom_call" | custom-call | tf_op jit(solution)/shard_map/pallas_call | solution.py:266
  56.9 0.7 %copy.17 = f32[3,512,64]{1,2,0:T(8,128)} copy(f32[3,512,64]{1,2,0:T(8,128)S(1)} %bitcast.4) | data formatting | bytes 786432
  57.7 1.1 %copy.18 = f32[3,64,2048]{2,1,0:T(8,128)} copy(f32[3,64,2048]{2,1,0:T(8,128)S(1)} %get-tuple-element.36) | data formatting | bytes 3145728
  58.8 0.7 %copy.19 = f32[3,128,128]{2,1,0:T(8,128)} copy(f32[3,128,128]{2,1,0:T(8,128)S(1)} %bitcast.5) | data formatting | bytes 393216
  (11 shorter events, 0.1 us)
Async XLA Ops:
  0.6 18.9 %copy-start = (bf16[512,2048]{1,0:T(8,128)(2,1)S(1)}, bf16[512,2048]{1,0:T(8,128)(2,1)}, u32[]{:S(2)}) copy-start(bf16[512,2048]{1,0:T(8,128)(2,1)} %rec.1) | copy-start | bytes 6291460
  0.6 18.9 %copy-start.2 = (bf16[128,512]{1,0:T(8,128)(2,1)S(1)}, bf16[128,512]{1,0:T(8,128)(2,1)}, u32[]{:S(2)}) copy-start(bf16[128,512]{1,0:T(8,128)(2,1)} %left_test.1) | copy-start | bytes 393220
  1.8 7.1 %collective-permute-start.1 = (bf16[512,128]{1,0:T(8,128)(2,1)S(1)}, bf16[512,128]{1,0:T(8,128)(2,1)S(1)}, u32[]{:S(2)}, u32[]{:S(2)}) collective-permute-start(bf16[512,128]{1,0:T(8,128)(2,1)S(1)} %get-tuple-element.22), channel_id=1, source_target_pairs={{1,0},{2,1},{3,2},{5,4},{6,5},{7,6},{9,8},{10,9},{11,10},{13,12},{... | collective-permute-start | bytes 393224 | tf_op jit(solution)/shard_map/ppermute | solution.py:23
  3.1 5.8 %collective-permute-start = (bf16[512,128]{1,0:T(8,128)(2,1)S(1)}, bf16[512,128]{1,0:T(8,128)(2,1)S(1)}, u32[]{:S(2)}, u32[]{:S(2)}) collective-permute-start(bf16[512,128]{1,0:T(8,128)(2,1)S(1)} %get-tuple-element.23), channel_id=1, source_target_pairs={{0,1},{1,2},{2,3},{4,5},{5,6},{6,7},{8,9},{9,10},{10,11},{12,13},{... | collective-permute-start | bytes 393224 | tf_op jit(solution)/shard_map/ppermute | solution.py:23
  9.0 10.5 %collective-permute-start.2 = (bf16[1,2304]{1,0:T(2,128)(2,1)S(1)}, bf16[1,2304]{1,0:T(2,128)(2,1)S(1)}, u32[]{:S(2)}, u32[]{:S(2)}) collective-permute-start(bf16[1,2304]{1,0:T(2,128)(2,1)S(1)} %pad_maximum_fusion.1), channel_id=1, source_target_pairs={{0,4},{4,8},{8,12},{12,16},{16,20},{20,24},{24,28},{1,5},{5,9},{9,... | collective-permute-start | bytes 13832 | tf_op jit(solution)/shard_map/ppermute | solution.py:23
  13.9 5.6 %collective-permute-start.3 = (bf16[1,2304]{1,0:T(2,128)(2,1)S(1)}, bf16[1,2304]{1,0:T(2,128)(2,1)S(1)}, u32[]{:S(2)}, u32[]{:S(2)}) collective-permute-start(bf16[1,2304]{1,0:T(2,128)(2,1)S(1)} %pad_maximum_fusion.2), channel_id=1, source_target_pairs={{4,0},{8,4},{12,8},{16,12},{20,16},{24,20},{28,24},{5,1},{9,5},{13... | collective-permute-start | bytes 13832 | tf_op jit(solution)/shard_map/ppermute | solution.py:23
  19.5 1.0 %copy-start.1 = (bf16[2048,128]{1,0:T(8,128)(2,1)S(1)}, bf16[2048,128]{1,0:T(8,128)(2,1)}, u32[]{:S(2)}) copy-start(bf16[2048,128]{1,0:T(8,128)(2,1)} %ctest.1) | copy-start | bytes 1572868

commit v3 on v2

v3 whole, which is shorter than its diff:
```python
import jax
import jax.numpy as jnp
from jax import lax
from jax.experimental import pallas as pl
from jax.experimental.pallas import tpu as pltpu
from jax.sharding import PartitionSpec as P

WIDE = 256
EDGE = 128
RIM = 16
F32 = jnp.float32
BF16 = jnp.bfloat16


def dot(a, b):
    return jnp.dot(a, b, preferred_element_type=F32)


def fused_kernel(
    rec, taps, gain, rtest, ctest, corange, left_test,
    strain, rout, yout, cout,
    padded, toep, right_test, gains, total,
    tm_send, tm_recv, rall, csend, call, y_send, y_recv, yall, yfull,
    tm_sems, r_sems, c_sems, call_sems, y_sems, yall_sems, halo_sems, own_sem,
):
    times, blocks = rall.shape[0], yall.shape[0]
    here_t, here_c = lax.axis_index("tm"), lax.axis_index("chan")
    bands, rank, rows = rout.shape
    samples = rec.shape[1]
    nr, nc = rall.shape[1], call.shape[1]
    span = padded.shape[1]
    corank = corange.shape[0]
    piece, width = corank // blocks, yall.shape[2]
    steps = samples // WIDE
    tail = EDGE + samples

    def peer(axis, d):
        if axis == "tm":
            return lax.rem(here_t + d, times)
        return lax.rem(here_c + d, blocks)

    def send(src, dst, sems, axis, d):
        copy = pltpu.make_async_remote_copy(
            src_ref=src, dst_ref=dst, send_sem=sems.at[0, d - 1], recv_sem=sems.at[1, d - 1],
            device_id={axis: peer(axis, d)}, device_id_type=pl.DeviceIdType.MESH,
        )
        copy.start()
        return copy

    around = [(c, t) for c in (-1, 0, 1) for t in (-1, 0, 1) if (c, t) != (0, 0)]

    def place(c, t):
        return {"chan": peer("chan", c + blocks), "tm": peer("tm", t + times)}

    barrier = pltpu.get_barrier_semaphore()
    for axis, count in (("tm", times), ("chan", blocks)):
        for d in range(1, count):
            pl.semaphore_signal(
                barrier, inc=1, device_id={axis: peer(axis, d)},
                device_id_type=pl.DeviceIdType.MESH,
            )
    for c, t in around:
        if c and t:
            pl.semaphore_signal(
                barrier, inc=1, device_id=place(c, t), device_id_type=pl.DeviceIdType.MESH
            )
    own = pltpu.make_async_copy(
        rec, padded.at[RIM : RIM + rows, EDGE : EDGE + samples], own_sem
    )
    own.start()
    pl.semaphore_wait(barrier, times + blocks - 2 + 4)
    row_from = {-1: slice(0, RIM), 0: slice(0, rows), 1: slice(rows - RIM, rows)}
    row_to = {-1: slice(RIM + rows, None), 0: slice(RIM, RIM + rows), 1: slice(0, RIM)}
    col_from = {-1: slice(0, EDGE), 0: slice(0, samples), 1: slice(samples - EDGE, samples)}
    col_to = {-1: slice(tail, span), 0: slice(EDGE, tail), 1: slice(0, EDGE)}
    row_to[-1] = slice(RIM + rows, rows + 2 * RIM)
    halos = []
    for i, (c, t) in enumerate(around):
        copy = pltpu.make_async_remote_copy(
            src_ref=rec.at[row_from[c], col_from[t]],
            dst_ref=padded.at[row_to[c], col_to[t]],
            send_sem=halo_sems.at[0, i], recv_sem=halo_sems.at[1, i],
            device_id=place(c, t), device_id_type=pl.DeviceIdType.MESH,
        )
        copy.start()
        halos.append(copy)

    for b in range(bands):
        spread = jnp.broadcast_to(taps[b : b + 1, :], (WIDE, 2 * WIDE))
        skewed = pltpu.roll(spread, 1, 1, stride=1, stride_axis=0)
        toep[b] = skewed.T.astype(BF16)
    right_test[:, 0:128] = ctest[...]
    turned = jnp.concatenate([rtest[...].astype(F32), jnp.zeros(rtest.shape, F32)], axis=0)
    right_test[:, 128:256] = turned.T.astype(BF16)
    column = jnp.broadcast_to(gain[...], (128, rows)).T
    gains[...] = jnp.concatenate([column, column], axis=1)
    total[...] = jnp.zeros_like(total)
    scaled = corange[...].astype(F32) * gain[...]
    lane = lax.broadcasted_iota(jnp.int32, scaled.shape, 1)
    weight = jnp.where(lane == 0, 0.0, pltpu.roll(scaled, 1, 1)) - jnp.where(
        lane == rows - 1, 0.0, pltpu.roll(scaled, rows - 1, 1)
    )
    top = weight.astype(BF16)
    rest = (weight - top.astype(F32)).astype(BF16)
    weight = jnp.concatenate([top, rest], axis=0)
    own.wait()
    for copy in halos:
        copy.wait()

    @pl.when(here_t == 0)
    def _():
        padded[:, 0:EDGE] = jnp.zeros((rows + 2 * RIM, EDGE), BF16)

    @pl.when(here_t == times - 1)
    def _():
        padded[:, tail:span] = jnp.zeros((rows + 2 * RIM, EDGE), BF16)

    @pl.when(here_c == 0)
    def _():
        padded[0:RIM, :] = jnp.zeros((RIM, span), BF16)

    @pl.when(here_c == blocks - 1)
    def _():
        padded[RIM + rows : rows + 2 * RIM, :] = jnp.zeros((RIM, span), BF16)

    both = dot(weight, padded[RIM : RIM + rows, :])
    before_row = padded[0:RIM, :].astype(F32)[RIM - 1 : RIM]
    after_row = padded[RIM + rows : rows + 2 * RIM, :].astype(F32)[0:1]
    yfull[...] = (
        both[:corank] + both[corank:]
        + scaled[:, rows - 1 : rows] * after_row - scaled[:, 0:1] * before_row
    )
    for p in range(blocks):
        block = yfull[p * piece : (p + 1) * piece, :]
        if width < span:
            block = jnp.concatenate(
                [block[:, k : k + width] for k in range(0, span, width)], axis=0
            )
        elif piece < RIM:
            block = jnp.concatenate([block, jnp.zeros((RIM - piece, span), F32)], axis=0)
        y_send[p] = block.astype(BF16)
    y_copies = [
        send(y_send.at[peer("chan", d)], y_recv.at[d - 1], y_sems, "chan", d)
        for d in range(1, blocks)
    ]

    def filter_step(step, carry):
        start = pl.multiple_of(step * WIDE, WIDE)
        window = padded[:, pl.ds(start, 2 * WIDE)]
        test = right_test[pl.ds(start, WIDE), :]
        for b in range(bands):
            filtered = dot(window, toep[b]).astype(BF16).astype(F32)
            after = pltpu.roll(filtered, filtered.shape[0] - 1, 0)
            before = pltpu.roll(filtered, 1, 0)
            value = (gains[...] * (after - before)[RIM : RIM + rows]).astype(BF16)
            strain[b, :, pl.ds(start, WIDE)] = value
            total[b] += dot(value, test)
        return carry

    half = (3 * steps) // 4
    lax.fori_loop(0, half, filter_step, 0)
    y_sum = y_send[here_c].astype(F32)
    for d in range(1, blocks):
        y_copies[d - 1].wait_recv()
        y_sum += y_recv[d - 1].astype(F32)
    yall[here_c] = y_sum.astype(BF16)
    yall_copies = [
        send(yall.at[here_c], yall.at[here_c], yall_sems, "chan", d) for d in range(1, blocks)
    ]

    lax.fori_loop(half, steps, filter_step, 0)

    for c in range(rows // 128):
        for b in range(bands):
            part = total[b, c * 128 : (c + 1) * 128, 128:256].T[:rank].astype(BF16)
            for k in range(rank // RIM):
                at = (c * bands + b) * rank + k * RIM
                row = at % nr
                tm_send[at // nr, row : row + RIM] = part[k * RIM : (k + 1) * RIM]
    order = left_test.shape[0]
    for b in range(bands):
        projected = total[b, :, 0:128]
        top = projected.astype(BF16)
        rest = (projected - top.astype(F32)).astype(BF16)
        term = (dot(left_test[...], top) + dot(left_test[...], rest)).astype(BF16)
        for k in range(order // RIM):
            at = b * order + k * RIM
            row = nr + at % nc
            tm_send[at // nc, row : row + RIM] = term[k * RIM : (k + 1) * RIM]
    tm_copies = [
        send(tm_send.at[peer("tm", d)], tm_recv.at[d - 1], tm_sems, "tm", d)
        for d in range(1, times)
    ]
    summed = tm_send[here_t].astype(F32)
    for d in range(1, times):
        tm_copies[d - 1].wait_recv()
        summed += tm_recv[d - 1].astype(F32)
    rall[here_t] = summed[0:nr].astype(BF16)
    call[here_c] = summed[nr : nr + nc].astype(BF16)
    c_copies = [
        send(call.at[here_c], call.at[here_c], call_sems, "chan", d) for d in range(1, blocks)
    ]
    r_copies = [send(rall.at[here_t], rall.at[here_t], r_sems, "tm", d) for d in range(1, times)]

    for copy in yall_copies:
        copy.wait_recv()
    for p in range(blocks):
        block = yall[p].astype(F32)[: piece * (span // width)]
        if width < span:
            block = jnp.concatenate(
                [block[k * piece : (k + 1) * piece] for k in range(span // width)], axis=1
            )
        yfull[p * piece : (p + 1) * piece, :] = block
    window = jnp.concatenate(
        [yfull[:, k : k + 2 * WIDE].astype(BF16) for k in range(0, samples, WIDE)], axis=0
    )
    for b in range(bands):
        result = dot(window, toep[b])
        for k in range(samples // WIDE):
            yout[b, :, k * WIDE : (k + 1) * WIDE] = result[k * corank : (k + 1) * corank]

    for copy in c_copies:
        copy.wait_recv()
    c_sum = call[0].astype(F32)
    for p in range(1, blocks):
        c_sum += call[p].astype(F32)
    csend[here_t] = c_sum
    core_copies = [
        send(csend.at[here_t], csend.at[here_t], c_sems, "tm", d) for d in range(1, times)
    ]

    for copy in r_copies:
        copy.wait_recv()
    per = nr // RIM
    for c in range(rows // 128):
        for b in range(bands):
            for k in range(rank // RIM):
                at = ((c * bands + b) * rank) // RIM + k
                part = rall[at // per, (at % per) * RIM : (at % per + 1) * RIM, :]
                rout[b, k * RIM : (k + 1) * RIM, c * 128 : (c + 1) * 128] = part.astype(F32)

    for copy in core_copies:
        copy.wait_recv()
    for q in range(times):
        cout[q * nc : (q + 1) * nc, :] = csend[q]
    for copy in tm_copies + y_copies + c_copies + r_copies + yall_copies + core_copies:
        copy.wait_send()


def on_device(recording, band_taps, channel_gain, range_test, corange_test, core_left, core_right):
    rows, samples = recording.shape
    bands, taps = band_taps.shape
    span = samples + 2 * EDGE
    rank, core_rank, corank = range_test.shape[1], core_left.shape[0], corange_test.shape[0]
    times, blocks = lax.axis_size("tm"), lax.axis_size("chan")
    nr, nc = bands * rank * rows // 128 // times, bands * core_rank // times
    piece = corank // blocks
    fold = max(1, RIM // piece)
    if span % (fold * 128):
        fold = 1
    tile = (max(RIM, piece), span // fold)
    vmem = pl.BlockSpec(memory_space=pltpu.VMEM)
    anywhere = pl.BlockSpec(memory_space=pl.ANY)

    def sems(count):
        return pltpu.SemaphoreType.DMA((2, count - 1))

    strain, ranges, corange_sketch, core_sketch = pl.pallas_call(
        fused_kernel,
        in_specs=[anywhere] + [vmem] * 6,
        out_specs=[vmem] * 4,
        out_shape=[
            jax.ShapeDtypeStruct((bands, rows, samples), BF16),
            jax.ShapeDtypeStruct((bands, rank, rows), F32),
            jax.ShapeDtypeStruct((bands, corank, samples), F32),
            jax.ShapeDtypeStruct((bands * core_rank, core_rank), F32),
        ],
        scratch_shapes=[
            pltpu.VMEM((rows + 2 * RIM, span), BF16),
            pltpu.VMEM((bands, 2 * WIDE, WIDE), BF16),
            pltpu.VMEM((samples, 256), BF16),
            pltpu.VMEM((rows, WIDE), F32),
            pltpu.VMEM((bands, rows, 256), F32),
            pltpu.VMEM((times, nr + nc, 128), BF16),
            pltpu.VMEM((times - 1, nr + nc, 128), BF16),
            pltpu.VMEM((times, nr, 128), BF16),
            pltpu.VMEM((times, nc, 128), F32),
            pltpu.VMEM((blocks, nc, 128), BF16),
            pltpu.VMEM((blocks,) + tile, BF16),
            pltpu.VMEM((blocks - 1,) + tile, BF16),
            pltpu.VMEM((blocks,) + tile, BF16),
            pltpu.VMEM((corank, span), F32),
            sems(times), sems(times), sems(times), sems(blocks), sems(blocks), sems(blocks),
            sems(9),
            pltpu.SemaphoreType.DMA,
        ],
        compiler_params=pltpu.CompilerParams(
            collective_id=0, has_side_effects=True, vmem_limit_bytes=36 * 2**20
        ),
    )(
        recording,
        jnp.pad(band_taps.astype(F32), ((0, 0), (0, 2 * WIDE - taps))),
        channel_gain[None, :],
        range_test.T,
        core_right,
        corange_test,
        core_left,
    )
    range_sketch = jnp.swapaxes(ranges, 1, 2)
    core_sketch = core_sketch.reshape(bands, core_rank, core_rank)
    return strain, range_sketch, corange_sketch, core_sketch


def solution(mesh):
    in_specs = (
        P("chan", "tm"),
        P(),
        P("chan"),
        P("tm", None),
        P(None, "chan"),
        P(None, "chan"),
        P("tm", None),
    )
    out_specs = (P(None, "chan", "tm"), P(None, "chan", None), P(None, None, "tm"), P())
    return jax.shard_map(
        on_device, mesh=mesh, in_specs=in_specs, out_specs=out_specs, check_vma=False
    )
```

time: 60 us -> 49.6 us (0.83)
  starting transfers between devices: 10.5 us -> 0 us
  local copies, waits for them, and re-layouts: 8.58 us -> 11.3 us
  waiting for transfers between devices: 2.13 us -> 0 us
    ppermute x4 -> x0, starting transfers between devices: 10.5 us -> none  [the longest x2 7.91 us: neighbours(): lax.ppermute(high_part, axis, forward)]
    unnamed x12 -> x16, local copies, waits for them, and re-layouts: 5.78 us -> 11.3 us
    ppermute x4 -> x0, waiting for transfers between devices: 2.13 us -> none  [the longest x2 2.12 us: neighbours(): lax.ppermute(low_part, axis, backward)]
    slice x4 -> x0, local copies, waits for them, and re-layouts: 1.95 us -> none  [the longest x1 1.14 us: on_device(): left, right = neighbours(recording[:, :EDGE], recording[:, -EDGE:], 'tm')]
    mul x1 -> x0, other arithmetic: 0.86 us -> none  [on_device(): scaled = corange_test.astype(F32) * channel_gain[None, :]]
    broadcast_in_dim x1 -> x0, local copies, waits for them, and re-layouts: 0.82 us -> none  [on_device(): channel_gain[:, None]]
    pad x1, other arithmetic: 0.08 us -> 0.69 us  [on_device(): jnp.pad(band_taps.astype(F32), ((0, 0), (0, 2 * WIDE - taps)))]
    pallas_call x2 -> x1, Pallas kernels: 36.4 us -> 36.7 us  [on_device(): pl.pallas_call(fused_kernel, in_specs=[anywhere] + [vmem] * 6, out_specs=...]
  transfers between devices with their start and end apart: 4 -> 0, of which waited for: 1 -> 0; matrix products, arithmetic and copies ran while one was open for 8% -> 0% of each run, Pallas kernels for 0% -> 0%
where the time goes in v3:
time: 49.6 us; the launch traced here: 49.3 us
  Pallas kernels  36.7 us (74%)
  local copies, waits for them, and re-layouts  11.3 us (23%)
  other arithmetic  0.69 us (1%)
  between operations  0.65 us (1%)
    pallas_call x1, Pallas kernels, on_device(): pl.pallas_call(fused_kernel, in_specs=[anywhere] + [vmem] * 6, out_specs=...  36.7 us
    unnamed x16, local copies, waits for them, and re-layouts  11.3 us

profile of v3, /device:TPU:0, one launch (start us, length us, event | category | flops | bytes accessed | tf_op | source)
XLA Modules:
  0.0 49.3 jit_solution(13928858885561438885)
XLA Ops:
  0.6 0.7 %pad_convert_fusion.taps = f32[3,512]{1,0:T(4,128)S(1)} fusion(bf16[3,255]{1,0:T(4,128)(2,1)} %param.8), kind=kLoop, calls=%fused_computation | loop fusion | flops 1536 | bytes 7674 | tf_op jit(solution)/shard_map/jit(_pad)/pad | solution.py:302
  1.3 0.0 copy-start
  1.3 1.6 %copy-done = bf16[512,2048]{1,0:T(8,128)(2,1)S(1)} copy-done((bf16[512,2048]{1,0:T(8,128)(2,1)S(1)}, bf16[512,2048]{1,0:T(8,128)(2,1)}, u32[]{:S(2)}) %copy-start) | copy-done | bytes 2097176
  2.9 0.0 copy-start.1
  2.9 1.0 %copy-done.1 = bf16[2048,128]{1,0:T(8,128)(2,1)S(1)} copy-done((bf16[2048,128]{1,0:T(8,128)(2,1)S(1)}, bf16[2048,128]{1,0:T(8,128)(2,1)}, u32[]{:S(2)}) %copy-start.1) | copy-done | bytes 524312
  4.0 0.0 copy-start.2
  4.0 0.9 %copy-done.2 = bf16[2048,64]{0,1:T(8,128)(2,1)S(1)} copy-done((bf16[2048,64]{0,1:T(8,128)(2,1)S(1)}, bf16[2048,64]{0,1:T(8,128)(2,1)}, u32[]{:S(2)}) %copy-start.2) | copy-done | bytes 262168
  4.9 0.0 copy-start.3
  4.9 0.9 %copy-done.3 = bf16[128,512]{1,0:T(8,128)(2,1)S(1)} copy-done((bf16[128,512]{1,0:T(8,128)(2,1)S(1)}, bf16[128,512]{1,0:T(8,128)(2,1)}, u32[]{:S(2)}) %copy-start.3) | copy-done | bytes 131096
  5.8 0.0 copy-start.4
  5.8 0.8 %copy-done.4 = bf16[64,512]{1,0:T(8,128)(2,1)S(1)} copy-done((bf16[64,512]{1,0:T(8,128)(2,1)S(1)}, bf16[64,512]{1,0:T(8,128)(2,1)}, u32[]{:S(2)}) %copy-start.4) | copy-done | bytes 65560
  6.6 0.0 copy-start.5
  6.6 0.7 %copy-done.5 = f32[512]{0:T(512)S(1)} copy-done((f32[512]{0:T(512)S(1)}, f32[512]{0:T(512)}, u32[]{:S(2)}) %copy-start.5) | copy-done | bytes 2072
  7.3 36.7 %shard_map.102 = (bf16[3,512,2048]{2,1,0:T(8,128)(2,1)S(1)}, f32[3,64,512]{2,1,0:T(8,128)S(1)}, f32[3,64,2048]{2,1,0:T(8,128)S(1)}, f32[384,128]{1,0:T(8,128)S(1)}) custom-call(bf16[512,2048]{1,0:T(8,128)(2,1)S(1)} %copy-done, f32[3,512]{1,0:T(4,128)S(1)} %pad_convert_fusion.taps, f32[1,512]{1,0:T(1,128)S(1)} %bitcast.7, bf16[64,2048]{1,0:T(8,128)(2,1)S(1)} %bitcast.5, ...), custom_call_target="tpu_custom_call" | custom-call | tf_op jit(solution)/shard_map/pallas_call | solution.py:268
  44.0 2.7 %copy.15 = bf16[3,512,2048]{2,1,0:T(8,128)(2,1)} copy(bf16[3,512,2048]{2,1,0:T(8,128)(2,1)S(1)} %get-tuple-element.16) | data formatting | bytes 12582912
  46.7 0.7 %copy.16 = f32[3,512,64]{1,2,0:T(8,128)} copy(f32[3,512,64]{1,2,0:T(8,128)S(1)} %bitcast.4) | data formatting | bytes 786432
  47.5 1.1 %copy.17 = f32[3,64,2048]{2,1,0:T(8,128)} copy(f32[3,64,2048]{2,1,0:T(8,128)S(1)} %get-tuple-element.18) | data formatting | bytes 3145728
  48.6 0.7 %copy.18 = f32[3,128,128]{2,1,0:T(8,128)} copy(f32[3,128,128]{2,1,0:T(8,128)S(1)} %bitcast.6) | data formatting | bytes 393216
Async XLA Ops:
  1.3 1.6 %copy-start = (bf16[512,2048]{1,0:T(8,128)(2,1)S(1)}, bf16[512,2048]{1,0:T(8,128)(2,1)}, u32[]{:S(2)}) copy-start(bf16[512,2048]{1,0:T(8,128)(2,1)} %rec.1) | copy-start | bytes 6291460
  2.9 1.0 %copy-start.1 = (bf16[2048,128]{1,0:T(8,128)(2,1)S(1)}, bf16[2048,128]{1,0:T(8,128)(2,1)}, u32[]{:S(2)}) copy-start(bf16[2048,128]{1,0:T(8,128)(2,1)} %ctest.1) | copy-start | bytes 1572868
  4.0 0.9 %copy-start.2 = (bf16[2048,64]{0,1:T(8,128)(2,1)S(1)}, bf16[2048,64]{0,1:T(8,128)(2,1)}, u32[]{:S(2)}) copy-start(bf16[2048,64]{0,1:T(8,128)(2,1)} %param.10) | copy-start | bytes 786436
  4.9 0.9 %copy-start.3 = (bf16[128,512]{1,0:T(8,128)(2,1)S(1)}, bf16[128,512]{1,0:T(8,128)(2,1)}, u32[]{:S(2)}) copy-start(bf16[128,512]{1,0:T(8,128)(2,1)} %left_test.1) | copy-start | bytes 393220
  5.8 0.8 %copy-start.4 = (bf16[64,512]{1,0:T(8,128)(2,1)S(1)}, bf16[64,512]{1,0:T(8,128)(2,1)}, u32[]{:S(2)}) copy-start(bf16[64,512]{1,0:T(8,128)(2,1)} %corange.1) | copy-start | bytes 196612
  6.6 0.7 %copy-start.5 = (f32[512]{0:T(512)S(1)}, f32[512]{0:T(512)}, u32[]{:S(2)}) copy-start(f32[512]{0:T(512)} %param.9) | copy-start | bytes 6148

commit v4 on v3

--- a/solution.py
+++ b/solution.py
@@ -17,17 +17,18 @@
 
 
 def fused_kernel(
-    rec, taps, gain, rtest, ctest, corange, left_test,
+    rec, taps, gain, rtest_hbm, ctest_hbm, corange_hbm, left_hbm,
     strain, rout, yout, cout,
-    padded, toep, right_test, gains, total,
+    padded, toep, right_test, gains, total, stage, out_sems,
     tm_send, tm_recv, rall, csend, call, y_send, y_recv, yall, yfull,
     tm_sems, r_sems, c_sems, call_sems, y_sems, yall_sems, halo_sems, own_sem,
+    rtest, ctest, corange, left_test, in_sems,
 ):
-    times, blocks = rall.shape[0], yall.shape[0]
+    times, blocks = rall.shape[1], yall.shape[0]
     here_t, here_c = lax.axis_index("tm"), lax.axis_index("chan")
     bands, rank, rows = rout.shape
     samples = rec.shape[1]
-    nr, nc = rall.shape[1], call.shape[1]
+    nr, nc = rall.shape[2], call.shape[2]
     span = padded.shape[1]
     corank = corange.shape[0]
     piece, width = corank // blocks, yall.shape[2]
@@ -39,9 +40,10 @@
             return lax.rem(here_t + d, times)
         return lax.rem(here_c + d, blocks)
 
-    def send(src, dst, sems, axis, d):
+    def send(src, dst, sems, axis, d, b=0):
+        at = b * ((times if axis == "tm" else blocks) - 1) + d - 1
         copy = pltpu.make_async_remote_copy(
-            src_ref=src, dst_ref=dst, send_sem=sems.at[0, d - 1], recv_sem=sems.at[1, d - 1],
+            src_ref=src, dst_ref=dst, send_sem=sems.at[0, at], recv_sem=sems.at[1, at],
             device_id={axis: peer(axis, d)}, device_id_type=pl.DeviceIdType.MESH,
         )
         copy.start()
@@ -68,6 +70,12 @@
         rec, padded.at[RIM : RIM + rows, EDGE : EDGE + samples], own_sem
     )
     own.start()
+    inputs = []
+    for i, (src, dst) in enumerate(
+        ((rtest_hbm, rtest), (ctest_hbm, ctest), (corange_hbm, corange), (left_hbm, left_test))
+    ):
+        inputs.append(pltpu.make_async_copy(src, dst, in_sems.at[i]))
+        inputs[-1].start()
     pl.semaphore_wait(barrier, times + blocks - 2 + 4)
     row_from = {-1: slice(0, RIM), 0: slice(0, rows), 1: slice(rows - RIM, rows)}
     row_to = {-1: slice(RIM + rows, None), 0: slice(RIM, RIM + rows), 1: slice(0, RIM)}
@@ -89,6 +97,8 @@
         spread = jnp.broadcast_to(taps[b : b + 1, :], (WIDE, 2 * WIDE))
         skewed = pltpu.roll(spread, 1, 1, stride=1, stride_axis=0)
         toep[b] = skewed.T.astype(BF16)
+    for copy in inputs:
+        copy.wait()
     right_test[:, 0:128] = ctest[...]
     turned = jnp.concatenate([rtest[...].astype(F32), jnp.zeros(rtest.shape, F32)], axis=0)
     right_test[:, 128:256] = turned.T.astype(BF16)
@@ -144,64 +154,112 @@
         for d in range(1, blocks)
     ]
 
-    def filter_step(step, carry):
-        start = pl.multiple_of(step * WIDE, WIDE)
-        window = padded[:, pl.ds(start, 2 * WIDE)]
-        test = right_test[pl.ds(start, WIDE), :]
-        for b in range(bands):
+    out_copies = []
+
+    def filter_band(b):
+        def filter_step(step, carry):
+            start = pl.multiple_of(step * WIDE, WIDE)
+            window = padded[:, pl.ds(start, 2 * WIDE)]
             filtered = dot(window, toep[b]).astype(BF16).astype(F32)
             after = pltpu.roll(filtered, filtered.shape[0] - 1, 0)
             before = pltpu.roll(filtered, 1, 0)
             value = (gains[...] * (after - before)[RIM : RIM + rows]).astype(BF16)
-            strain[b, :, pl.ds(start, WIDE)] = value
-            total[b] += dot(value, test)
-        return carry
-
-    half = (3 * steps) // 4
-    lax.fori_loop(0, half, filter_step, 0)
-    y_sum = y_send[here_c].astype(F32)
-    for d in range(1, blocks):
-        y_copies[d - 1].wait_recv()
-        y_sum += y_recv[d - 1].astype(F32)
-    yall[here_c] = y_sum.astype(BF16)
-    yall_copies = [
-        send(yall.at[here_c], yall.at[here_c], yall_sems, "chan", d) for d in range(1, blocks)
-    ]
-
-    lax.fori_loop(half, steps, filter_step, 0)
-
-    for c in range(rows // 128):
-        for b in range(bands):
+            stage[b, :, pl.ds(start, WIDE)] = value
+            total[b] += dot(value, right_test[pl.ds(start, WIDE), :])
+            return carry
+
+        lax.fori_loop(0, steps, filter_step, 0)
+        out_copies.append(pltpu.make_async_copy(stage.at[b], strain.at[b], out_sems.at[b]))
+        out_copies[-1].start()
+
+    started = []
+
+    def spread_terms(b):
+        for c in range(rows // 128):
             part = total[b, c * 128 : (c + 1) * 128, 128:256].T[:rank].astype(BF16)
             for k in range(rank // RIM):
-                at = (c * bands + b) * rank + k * RIM
+                at = c * rank + k * RIM
                 row = at % nr
-                tm_send[at // nr, row : row + RIM] = part[k * RIM : (k + 1) * RIM]
-    order = left_test.shape[0]
-    for b in range(bands):
+                tm_send[b, at // nr, row : row + RIM] = part[k * RIM : (k + 1) * RIM]
         projected = total[b, :, 0:128]
         top = projected.astype(BF16)
         rest = (projected - top.astype(F32)).astype(BF16)
         term = (dot(left_test[...], top) + dot(left_test[...], rest)).astype(BF16)
-        for k in range(order // RIM):
-            at = b * order + k * RIM
+        for k in range(left_test.shape[0] // RIM):
+            at = k * RIM
             row = nr + at % nc
-            tm_send[at // nc, row : row + RIM] = term[k * RIM : (k + 1) * RIM]
-    tm_copies = [
-        send(tm_send.at[peer("tm", d)], tm_recv.at[d - 1], tm_sems, "tm", d)
-        for d in range(1, times)
-    ]
-    summed = tm_send[here_t].astype(F32)
-    for d in range(1, times):
-        tm_copies[d - 1].wait_recv()
-        summed += tm_recv[d - 1].astype(F32)
-    rall[here_t] = summed[0:nr].astype(BF16)
-    call[here_c] = summed[nr : nr + nc].astype(BF16)
-    c_copies = [
-        send(call.at[here_c], call.at[here_c], call_sems, "chan", d) for d in range(1, blocks)
-    ]
-    r_copies = [send(rall.at[here_t], rall.at[here_t], r_sems, "tm", d) for d in range(1, times)]
-
+            tm_send[b, at // nc, row : row + RIM] = term[k * RIM : (k + 1) * RIM]
+        copies = [
+            send(tm_send.at[b, peer("tm", d)], tm_recv.at[b, d - 1], tm_sems, "tm", d, b)
+            for d in range(1, times)
+        ]
+        started.extend(copies)
+        return copies
+
+    def sum_terms(b, copies):
+        summed = tm_send[b, here_t].astype(F32)
+        for d in range(1, times):
+            copies[d - 1].wait_recv()
+            summed += tm_recv[b, d - 1].astype(F32)
+        rall[b, here_t] = summed[0:nr].astype(BF16)
+        call[b, here_c] = summed[nr : nr + nc].astype(BF16)
+        over_c = [
+            send(call.at[b, here_c], call.at[b, here_c], call_sems, "chan", d, b)
+            for d in range(1, blocks)
+        ]
+        over_t = [
+            send(rall.at[b, here_t], rall.at[b, here_t], r_sems, "tm", d, b)
+            for d in range(1, times)
+        ]
+        started.extend(over_c + over_t)
+        return over_c, over_t
+
+    def sum_core(b, copies):
+        for copy in copies:
+            copy.wait_recv()
+        c_sum = call[b, 0].astype(F32)
+        for p in range(1, blocks):
+            c_sum += call[b, p].astype(F32)
+        csend[b, here_t] = c_sum
+        over_t = [
+            send(csend.at[b, here_t], csend.at[b, here_t], c_sems, "tm", d, b)
+            for d in range(1, times)
+        ]
+        started.extend(over_t)
+        return over_t
+
+    def store_range(b, copies):
+        for copy in copies:
+            copy.wait_recv()
+        for c in range(rows // 128):
+            for k in range(rank // RIM):
+                at = c * rank + k * RIM
+                part = rall[b, at // nr, at % nr : at % nr + RIM, :]
+                rout[b, k * RIM : (k + 1) * RIM, c * 128 : (c + 1) * 128] = part.astype(F32)
+
+    terms, sums, cores = {}, {}, {}
+    for b in range(bands):
+        filter_band(b)
+        terms[b] = spread_terms(b)
+        if b == 0:
+            y_sum = y_send[here_c].astype(F32)
+            for d in range(1, blocks):
+                y_copies[d - 1].wait_recv()
+                y_sum += y_recv[d - 1].astype(F32)
+            yall[here_c] = y_sum.astype(BF16)
+            yall_copies = [
+                send(yall.at[here_c], yall.at[here_c], yall_sems, "chan", d) for d in range(1, blocks)
+            ]
+        if b >= 1:
+            sums[b - 1] = sum_terms(b - 1, terms[b - 1])
+        if b >= 2:
+            cores[b - 2] = sum_core(b - 2, sums[b - 2][0])
+    final = bands - 1
+    sums[final] = sum_terms(final, terms[final])
+    for b in range(max(bands - 2, 0), final):
+        cores[b] = sum_core(b, sums[b][0])
+    for b in range(final):
+        store_range(b, sums[b][1])
     for copy in yall_copies:
         copy.wait_recv()
     for p in range(blocks):
@@ -219,32 +277,17 @@
         for k in range(samples // WIDE):
             yout[b, :, k * WIDE : (k + 1) * WIDE] = result[k * corank : (k + 1) * corank]
 
-    for copy in c_copies:
-        copy.wait_recv()
-    c_sum = call[0].astype(F32)
-    for p in range(1, blocks):
-        c_sum += call[p].astype(F32)
-    csend[here_t] = c_sum
-    core_copies = [
-        send(csend.at[here_t], csend.at[here_t], c_sems, "tm", d) for d in range(1, times)
-    ]
-
-    for copy in r_copies:
-        copy.wait_recv()
-    per = nr // RIM
-    for c in range(rows // 128):
-        for b in range(bands):
-            for k in range(rank // RIM):
-                at = ((c * bands + b) * rank) // RIM + k
-                part = rall[at // per, (at % per) * RIM : (at % per + 1) * RIM, :]
-                rout[b, k * RIM : (k + 1) * RIM, c * 128 : (c + 1) * 128] = part.astype(F32)
-
-    for copy in core_copies:
-        copy.wait_recv()
-    for q in range(times):
-        cout[q * nc : (q + 1) * nc, :] = csend[q]
-    for copy in tm_copies + y_copies + c_copies + r_copies + yall_copies + core_copies:
+    cores[final] = sum_core(final, sums[final][0])
+    store_range(final, sums[final][1])
+    for b in range(bands):
+        for copy in cores[b]:
+            copy.wait_recv()
+        for q in range(times):
+            cout[b * times * nc + q * nc : b * times * nc + (q + 1) * nc, :] = csend[b, q]
+    for copy in started + y_copies + yall_copies:
         copy.wait_send()
+    for copy in out_copies:
+        copy.wait()
 
 
 def on_device(recording, band_taps, channel_gain, range_test, corange_test, core_left, core_right):
@@ -253,22 +296,22 @@
     span = samples + 2 * EDGE
     rank, core_rank, corank = range_test.shape[1], core_left.shape[0], corange_test.shape[0]
     times, blocks = lax.axis_size("tm"), lax.axis_size("chan")
-    nr, nc = bands * rank * rows // 128 // times, bands * core_rank // times
+    nr, nc = rank * rows // 128 // times, core_rank // times
     piece = corank // blocks
     fold = max(1, RIM // piece)
     if span % (fold * 128):
         fold = 1
     tile = (max(RIM, piece), span // fold)
     vmem = pl.BlockSpec(memory_space=pltpu.VMEM)
-    anywhere = pl.BlockSpec(memory_space=pl.ANY)
-
-    def sems(count):
-        return pltpu.SemaphoreType.DMA((2, count - 1))
+    anywhere = pl.BlockSpec(memory_space=pltpu.HBM)
+
+    def sems(count, parts=1):
+        return pltpu.SemaphoreType.DMA((2, parts * (count - 1)))
 
     strain, ranges, corange_sketch, core_sketch = pl.pallas_call(
         fused_kernel,
-        in_specs=[anywhere] + [vmem] * 6,
-        out_specs=[vmem] * 4,
+        in_specs=[anywhere] + [vmem] * 2 + [anywhere] * 4,
+        out_specs=[anywhere] + [vmem] * 3,
         out_shape=[
             jax.ShapeDtypeStruct((bands, rows, samples), BF16),
             jax.ShapeDtypeStruct((bands, rank, rows), F32),
@@ -281,21 +324,29 @@
             pltpu.VMEM((samples, 256), BF16),
             pltpu.VMEM((rows, WIDE), F32),
             pltpu.VMEM((bands, rows, 256), F32),
-            pltpu.VMEM((times, nr + nc, 128), BF16),
-            pltpu.VMEM((times - 1, nr + nc, 128), BF16),
-            pltpu.VMEM((times, nr, 128), BF16),
-            pltpu.VMEM((times, nc, 128), F32),
-            pltpu.VMEM((blocks, nc, 128), BF16),
+            pltpu.VMEM((bands, rows, samples), BF16),
+            pltpu.SemaphoreType.DMA((bands,)),
+            pltpu.VMEM((bands, times, nr + nc, 128), BF16),
+            pltpu.VMEM((bands, times - 1, nr + nc, 128), BF16),
+            pltpu.VMEM((bands, times, nr, 128), BF16),
+            pltpu.VMEM((bands, times, nc, 128), F32),
+            pltpu.VMEM((bands, blocks, nc, 128), BF16),
             pltpu.VMEM((blocks,) + tile, BF16),
             pltpu.VMEM((blocks - 1,) + tile, BF16),
             pltpu.VMEM((blocks,) + tile, BF16),
             pltpu.VMEM((corank, span), F32),
-            sems(times), sems(times), sems(times), sems(blocks), sems(blocks), sems(blocks),
+            sems(times, bands), sems(times, bands), sems(times, bands), sems(blocks, bands),
+            sems(blocks), sems(blocks),
             sems(9),
             pltpu.SemaphoreType.DMA,
+            pltpu.VMEM((rank, samples), BF16),
+            pltpu.VMEM((samples, core_rank), BF16),
+            pltpu.VMEM((corank, rows), BF16),
+            pltpu.VMEM((core_rank, rows), BF16),
+            pltpu.SemaphoreType.DMA((4,)),
         ],
         compiler_params=pltpu.CompilerParams(
-            collective_id=0, has_side_effects=True, vmem_limit_bytes=36 * 2**20
+            collective_id=0, has_side_effects=True, vmem_limit_bytes=55 * 2**20
         ),
     )(
         recording,

time: 49.6 us -> 54 us (1.089)
  Pallas kernels: 36.7 us -> 42.4 us
  local copies, waits for them, and re-layouts: 11.3 us -> 9.33 us
  other arithmetic: 0.69 us -> 1.28 us
    pallas_call x1, Pallas kernels: 36.7 us -> 42.4 us  [on_device(): pl.pallas_call(fused_kernel, in_specs=[anywhere] + [vmem] * 2 + [anywhere...]
    unnamed x16 -> x10, local copies, waits for them, and re-layouts: 11.3 us -> 9.33 us
    pad x1, other arithmetic: 0.69 us -> 1.28 us  [on_device(): jnp.pad(band_taps.astype(F32), ((0, 0), (0, 2 * WIDE - taps)))]
where the time goes in v4:
time: 54 us; the launch traced here: 53.7 us
  Pallas kernels  42.4 us (79%)
  local copies, waits for them, and re-layouts  9.33 us (17%)
  other arithmetic  1.28 us (2%)
  between operations  0.66 us (1%)
    pallas_call x1, Pallas kernels, on_device(): pl.pallas_call(fused_kernel, in_specs=[anywhere] + [vmem] * 2 + [anywhere...  42.4 us
    unnamed x10, local copies, waits for them, and re-layouts  9.33 us
    pad x1, other arithmetic, on_device(): jnp.pad(band_taps.astype(F32), ((0, 0), (0, 2 * WIDE - taps)))  1.28 us

profile of v4, /device:TPU:0, one launch (start us, length us, event | category | flops | bytes accessed | tf_op | source)
XLA Modules:
  0.0 53.7 jit_solution(15800813246790962075)
XLA Ops:
  0.6 1.3 %pad_convert_fusion.taps = f32[3,512]{1,0:T(4,128)} fusion(bf16[3,255]{1,0:T(4,128)(2,1)} %param.8), kind=kLoop, calls=%fused_computation | loop fusion | flops 1536 | bytes 7674 | tf_op jit(solution)/shard_map/jit(_pad)/pad | solution.py:353
  1.9 42.4 %shard_map.102 = (bf16[3,512,2048]{2,1,0:T(8,128)(2,1)}, f32[3,64,512]{2,1,0:T(8,128)}, f32[3,64,2048]{2,1,0:T(8,128)}, f32[384,128]{1,0:T(8,128)}) custom-call(bf16[512,2048]{1,0:T(8,128)(2,1)} %rec.1, f32[3,512]{1,0:T(4,128)} %pad_convert_fusion.taps, f32[1,512]{1,0:T(1,128)} %bitcast.7, bf16[64,2048]{1,0:T(8,128)(2,1)} %bitcast.5, ...), custom_call_target="tpu_custom_call" | custom-call | tf_op jit(solution)/shard_map/pallas_call | solution.py:311
  44.4 0.0 copy-start.1
  44.4 0.0 copy-start
  44.4 6.8 %copy.15 = bf16[3,512,2048]{2,1,0:T(8,128)(2,1)} copy(bf16[3,512,2048]{2,1,0:T(8,128)(2,1)} %get-tuple-element.16) | data formatting | bytes 12582912
  51.1 0.0 copy-done.1
  51.1 0.0 copy-start.2
  51.1 0.7 %copy.16 = f32[3,512,64]{1,2,0:T(8,128)} copy(f32[3,512,64]{1,2,0:T(8,128)S(1)} %bitcast.4) | data formatting | bytes 786432
  51.9 0.0 copy-done
  51.9 1.1 %copy.17 = f32[3,64,2048]{2,1,0:T(8,128)} copy(f32[3,64,2048]{2,1,0:T(8,128)S(1)} %copy-done) | data formatting | bytes 3145728
  53.0 0.0 copy-done.2
  53.0 0.7 %copy.18 = f32[3,128,128]{2,1,0:T(8,128)} copy(f32[3,128,128]{2,1,0:T(8,128)S(1)} %bitcast.6) | data formatting | bytes 393216
Async XLA Ops:
  44.4 6.8 %copy-start.1 = (f32[3,64,512]{2,1,0:T(8,128)S(1)}, f32[3,64,512]{2,1,0:T(8,128)}, u32[]{:S(2)}) copy-start(f32[3,64,512]{2,1,0:T(8,128)} %get-tuple-element.9) | copy-start | bytes 1179652
  44.4 7.5 %copy-start = (f32[3,64,2048]{2,1,0:T(8,128)S(1)}, f32[3,64,2048]{2,1,0:T(8,128)}, u32[]{:S(2)}) copy-start(f32[3,64,2048]{2,1,0:T(8,128)} %get-tuple-element.18) | copy-start | bytes 4718596
  51.1 1.9 %copy-start.2 = (f32[384,128]{1,0:T(8,128)S(1)}, f32[384,128]{1,0:T(8,128)}, u32[]{:S(2)}) copy-start(f32[384,128]{1,0:T(8,128)} %get-tuple-element.11) | copy-start | bytes 589828
